TPU v7x, 32 devices: a whole 2x2x4 slice. The times are simulated.
32 devices in a mesh: tok: 8 (over z, x), head: 4 (over y, core).
Axes of the slice: x: 2, y: 2, z: 4, core: 2. Of those that a mesh axis runs over, the one named last changes fastest.
Arguments:
- queries: bfloat16 [8192, 4096], P(('tok', 'head')), may hold values from -32 to 32
- key_states: bfloat16 [8192, 512], P(('tok', 'head')), may hold values from -10 to 10
- value_states: bfloat16 [8192, 512], P(('tok', 'head')), may hold values from -6 to 6
- out_grad: bfloat16 [8192, 4096], P(('tok', 'head')), may hold values from -15 to 15
- sink_logits: float32 [64], P('head'), may hold values from 0 to 5
- branch_start: int32 [16], replicated, may hold values from 0 to 8064, as said below
- branch_len: int32 [16], replicated, may hold values from 128 to 384, as said below
- parent_list: int32 [16, 2], replicated, may hold values from -1 to 256, as said below
Outputs:
- attn_out: bfloat16 [8192, 4096], P(('tok', 'head'))
- query_grad: bfloat16 [8192, 4096], P(('tok', 'head'))
- key_grad: bfloat16 [8192, 512], P(('tok', 'head'))
- value_grad: bfloat16 [8192, 512], P(('tok', 'head'))
- sink_grad: float32 [64], P('head')
Inputs may be any that keep to these rules, and one draw needn't show every extreme that they name: `branch_start`: branch b lies within the tokens of index b // 2 of tok. The branches of one index follow one another in order, begin at multiples of 128 and do not intersect; tokens between them belong to no branch. `branch_len`: A multiple of 128. `parent_list`: row b is (parent branch, tail offset). The branches of index 0 of tok have parent -1 and offset 0; the parent of a branch on index d lies on index d - s for some s from 1 to min(3, d), and each s from 1 to 3 occurs. Branches 2m and 2m + 1 are siblings with equal rows. The offset is a multiple of 128 and the 128 tokens of the parent that begin there lie inside the parent.
All inputs are finite; a program needn't handle non-finite values.
Results may differ from a plain program's by a relative error of at most 0.02.
Values may be sent and summed in bfloat16 or wider, within the bound.
No kernel may reach another device: no remote copies, remote signals or barrier semaphores. Data moves between devices by JAX's collectives and lax.ppermute only.
A program may use at most 64 MiB of HBM per device.

v0:
```python
import functools

import jax
import jax.numpy as jnp
from jax import lax
from jax.experimental import pallas as pl
from jax.experimental.pallas import tpu as pltpu
from jax.sharding import PartitionSpec as P

HEAD_DIM = 64
KV_HEADS = 8
GROUP = 8
WINDOW = 128
LAG = 3
BR_DEV = 2
PAIRS = KV_HEADS // 2
FACTOR = 0.125
LOW = -1e30
EXTRA = 16
BF16 = jnp.bfloat16
F32 = jnp.float32

SMEM = pl.BlockSpec(memory_space=pltpu.SMEM)
VMEM = pl.BlockSpec(memory_space=pltpu.VMEM)
PARAMS = pltpu.CompilerParams(vmem_limit_bytes=24 * 1024 * 1024)


def shift(value, axis, steps):
    count = lax.axis_size(axis)
    leading, last = (max(0, -steps), min(count, count - steps))
    return lax.ppermute(value, axis, [(source, source + steps) for source in range(leading, last)])


def ring(value, axis, steps):
    count = lax.axis_size(axis)
    return lax.ppermute(value, axis, [(source, (source + steps) % count) for source in range(count)])


def row_split(row, dims):
    high = row.astype(BF16).astype(F32)
    middle = (row - high).astype(BF16).astype(F32)
    low = row - high - middle
    place = lax.broadcasted_iota(jnp.int32, dims, 0)
    rest = jnp.where(place == 2, low, 0.0)
    return jnp.where(place == 0, high, jnp.where(place == 1, middle, rest)).astype(BF16)


def row_join(rows):
    rows = rows.astype(F32)
    return rows[0:1] + rows[1:2] + rows[2:3]


def child_tail(table, tok, distance, tok_count, blocks):
    branches = tok_count * BR_DEV
    child = jnp.minimum(tok + distance, tok_count - 1) * BR_DEV
    parent = table[2 * branches + child]
    safe = jnp.maximum(parent, 0)
    valid = (tok + distance < tok_count) & (parent >= 0) & (safe // BR_DEV == tok)
    place = (table[safe] + table[3 * branches + child]) // WINDOW - tok * blocks
    return valid, jnp.where(valid, place, 0)


def block_state(table, tok, tok_count, block):
    branches = tok_count * BR_DEV
    position = block * WINDOW
    alive, opening = jnp.bool_(False), jnp.bool_(False)
    for branch in range(BR_DEV):
        start = table[tok * BR_DEV + branch]
        length = table[branches + tok * BR_DEV + branch]
        alive = alive | ((start <= position) & (position < start + length))
        opening = opening | (start == position)
    has_tail = table[2 * branches + tok * BR_DEV] >= 0
    return alive, opening, jnp.logical_not(opening) | has_tail


def pack_kernel(sinks, key_ref, value_ref, slot_ref, halo_ref):
    slots, rows = slot_ref.shape[0], key_ref.shape[0]
    width = KV_HEADS * HEAD_DIM // slots
    lane = lax.broadcasted_iota(jnp.int32, (1, 2 * width), 1)
    sink_row = jnp.zeros((1, 2 * width), F32)
    for head in range(sinks.shape[0]):
        sink_row = jnp.where(lane == head, sinks[head], sink_row)
    extra = row_split(sink_row, (EXTRA, 2 * width))
    for slot in range(slots):
        lanes = slice(slot * width, (slot + 1) * width)
        slot_ref[slot, :rows] = jnp.concatenate([key_ref[:, lanes], value_ref[:, lanes]], axis=1)
        slot_ref[slot, rows:] = extra
    for pair in range(PAIRS):
        lanes = slice(pair * 128, (pair + 1) * 128)
        last = slice(rows - WINDOW, rows)
        halo_ref[pair] = jnp.concatenate([key_ref[last, lanes], value_ref[last, lanes]], axis=1)


def choose_kernel(tok_count, blocks, table, all_ref, *refs):
    tok = lax.axis_index("tok")
    *out_refs, sink_ref = refs
    slots = all_ref.shape[0]
    rows = all_ref.shape[1] - EXTRA
    blocks_here = rows // WINDOW
    heads = sink_ref.shape[0] // slots
    for distance, out_ref in enumerate(out_refs, 1):
        _, place = child_tail(table, tok, distance, tok_count, blocks)
        begin = pl.multiple_of(place % blocks_here * WINDOW, WINDOW)
        out_ref[...] = all_ref[place // blocks_here, pl.ds(begin, WINDOW), :]
    for slot in range(slots):
        sink_row = row_join(all_ref[slot, rows:, :])[:, :128]
        turned = jnp.broadcast_to(sink_row, (128, 128)).T
        sink_ref[slot * heads : (slot + 1) * heads, :] = turned[:heads]


def arrive_kernel(tok_count, table, *refs):
    tok = lax.axis_index("tok")
    *in_refs, out_ref = refs
    parent = table[2 * tok_count * BR_DEV + tok * BR_DEV]
    mine = jnp.where(parent >= 0, tok - jnp.maximum(parent, 0) // BR_DEV, 1)
    for distance, in_ref in enumerate(in_refs, 1):

        @pl.when(mine == distance)
        def _(in_ref=in_ref):
            out_ref[...] = in_ref[...]


def attend_kernel(
    tok_count,
    per_slot,
    blocks_here,
    table,
    sink_ref,
    q_ref,
    g_ref,
    k_ref,
    v_ref,
    halo_ref,
    tail_ref,
    o_ref,
    dq_ref,
    dk_ref,
    dv_ref,
    dhalo_ref,
    dtail_ref,
    tail_sum,
    sink_rows,
    q_turned,
    g_turned,
    prob2,
    slope2,
):
    pair, block = pl.program_id(0), pl.program_id(1)
    tok, head = lax.axis_index("tok"), lax.axis_index("head")
    number = (tok * lax.axis_size("head") + head) * blocks_here + block
    alive, opening, prev_ok = block_state(table, tok, tok_count, number)
    here = pl.ds(pl.multiple_of(block * WINDOW, WINDOW), WINDOW)
    before = pl.ds(pl.multiple_of(jnp.maximum(block - 1, 0) * WINDOW, WINDOW), WINDOW)
    first = block == 0

    @pl.when(first)
    def _():
        tail_sum[...] = jnp.zeros_like(tail_sum)
        dhalo_ref[...] = jnp.zeros_like(dhalo_ref)
        sink_rows[...] = jnp.zeros_like(sink_rows)

    @pl.when(jnp.logical_not(alive))
    def _():
        o_ref[...] = jnp.zeros_like(o_ref)
        dq_ref[...] = jnp.zeros_like(dq_ref)
        dk_ref[here, :] = jnp.zeros((WINDOW, 128), F32)
        dv_ref[here, :] = jnp.zeros((WINDOW, 128), F32)

    @pl.when(alive)
    def _():
        halo = halo_ref[0]
        if per_slot == 2:
            tail = tail_ref[0]
            tail_k, tail_v = tail[:, :128], tail[:, 128:]
        else:
            tail_k = jnp.concatenate([tail_ref[0][:, :64], tail_ref[1][:, :64]], axis=1)
            tail_v = jnp.concatenate([tail_ref[0][:, 64:], tail_ref[1][:, 64:]], axis=1)
        near_k = jnp.where(first, halo[:, :128], k_ref[before, :])
        near_v = jnp.where(first, halo[:, 128:], v_ref[before, :])
        prev_k = jnp.where(opening, tail_k, near_k)
        prev_v = jnp.where(opening, tail_v, near_v)
        both_k = jnp.concatenate([k_ref[here, :], prev_k], axis=0) * BF16(FACTOR)
        both_v = jnp.concatenate([v_ref[here, :], prev_v], axis=0)
        turned_k, turned_v = both_k.T, both_v.T
        bias = jnp.where(prev_ok, 0.0, LOW)
        key_place = lax.broadcasted_iota(jnp.int32, (WINDOW, WINDOW), 0)
        query_place = lax.broadcasted_iota(jnp.int32, (WINDOW, WINDOW), 1)
        own_one = key_place <= query_place
        own = jnp.concatenate([own_one, own_one], axis=1)
        own16 = own.astype(F32).astype(BF16)
        turn = (((1,), (1,)), ((), ()))
        couples = GROUP // 2

        def columns(index):
            return slice(index * 128, (index + 1) * 128)

        def wide(index):
            return slice(index * 256, (index + 1) * 256)

        def feats(index):
            unit = index // couples
            return slice(unit * HEAD_DIM, (unit + 1) * HEAD_DIM)

        def products(index):
            q_t, g_t = q_ref[:, columns(index)].T, g_ref[:, columns(index)].T
            q_t = jnp.concatenate([q_t[:64], q_t[64:]], axis=1)
            g_t = jnp.concatenate([g_t[:64], g_t[64:]], axis=1)
            q_turned[:, wide(index)] = q_t
            g_turned[:, wide(index)] = g_t
            score2 = jnp.dot(both_k[:, feats(index)], q_t, preferred_element_type=F32)
            dp2 = jnp.dot(both_v[:, feats(index)], g_t, preferred_element_type=F32)
            score = jnp.where(own, score2[:WINDOW], score2[WINDOW:] + bias)
            return score, jnp.where(own, dp2[:WINDOW], dp2[WINDOW:])

        def weigh(index, score, dp):
            row = index * 2
            sink = jnp.concatenate([sink_ref[row : row + 1], sink_ref[row + 1 : row + 2]], axis=1)
            peak = jnp.maximum(jnp.max(score, axis=0, keepdims=True), sink)
            weight = jnp.exp(score - peak)
            sink_weight = jnp.exp(sink - peak)
            inverse = 1.0 / (jnp.sum(weight, axis=0, keepdims=True) + sink_weight)
            prob = weight * inverse
            term = prob * dp
            delta = jnp.sum(term, axis=0, keepdims=True)
            prob16 = prob.astype(BF16)
            slope16 = (term - prob * delta).astype(BF16)
            prob_own, slope_own = prob16 * own16, slope16 * own16
            prob2[:WINDOW, wide(index)] = prob_own
            prob2[WINDOW:, wide(index)] = prob16 - prob_own
            slope2[:WINDOW, wide(index)] = slope_own
            slope2[WINDOW:, wide(index)] = slope16 - slope_own
            sink_term = sink_weight * inverse * delta
            sink_rows[row : row + 1] += sink_term[:, :WINDOW]
            sink_rows[row + 1 : row + 2] += sink_term[:, WINDOW:]

        def finish(index):
            for source, turned, out_ref in ((prob2, turned_v, o_ref), (slope2, turned_k, dq_ref)):
                out_t = jnp.dot(
                    turned[feats(index)], source[:, wide(index)], preferred_element_type=F32
                ).astype(BF16)
                out_ref[:, columns(index)] = jnp.concatenate(
                    [out_t[:, :128], out_t[:, 128:]], axis=0
                ).T

        def reduce(unit):
            lanes = slice(unit * couples * 256, (unit + 1) * couples * 256)
            dk = lax.dot_general(
                slope2[:, lanes], q_turned[:, lanes], turn, preferred_element_type=F32
            )
            dv = lax.dot_general(
                prob2[:, lanes], g_turned[:, lanes], turn, preferred_element_type=F32
            )
            return dk * FACTOR, dv

        total = 2 * couples
        ahead = {0: products(0)}
        grads = []
        for index in range(total):
            if index + 1 < total:
                ahead[index + 1] = products(index + 1)
            weigh(index, *ahead.pop(index))
            if index >= 1:
                finish(index - 1)
            if index == couples:
                grads.append(reduce(0))
        finish(total - 1)
        grads.append(reduce(1))
        dk = jnp.concatenate([grads[0][0], grads[1][0]], axis=1)
        dv = jnp.concatenate([grads[0][1], grads[1][1]], axis=1)
        dk_ref[here, :] = dk[:WINDOW]
        dv_ref[here, :] = dv[:WINDOW]

        @pl.when(opening & prev_ok)
        def _():
            tail_sum[:, :128] += dk[WINDOW:]
            tail_sum[:, 128:] += dv[WINDOW:]

        @pl.when(jnp.logical_not(opening) & first)
        def _():
            dhalo_ref[0, :, :128] = dk[WINDOW:].astype(BF16)
            dhalo_ref[0, :, 128:] = dv[WINDOW:].astype(BF16)

        @pl.when(jnp.logical_not(opening) & jnp.logical_not(first))
        def _():
            dk_ref[before, :] += dk[WINDOW:]
            dv_ref[before, :] += dv[WINDOW:]

    @pl.when(block == blocks_here - 1)
    def _():
        slots, width = dtail_ref.shape[0], dtail_ref.shape[2]
        heads = 2 * GROUP // slots
        total = tail_sum[...].astype(BF16)
        for slot in range(slots):
            feats = slice(slot * width // 2, (slot + 1) * width // 2)
            dtail_ref[slot, :WINDOW] = jnp.concatenate(
                [total[:, :128][:, feats], total[:, 128:][:, feats]], axis=1
            )
            rows = sink_rows[slot * heads : (slot + 1) * heads]
            rows = jnp.concatenate([rows, jnp.zeros((128 - heads, WINDOW), F32)], axis=0)
            sink_row = jnp.sum(rows.T, axis=0, keepdims=True)
            if width > 128:
                sink_row = jnp.concatenate([sink_row, jnp.zeros((1, width - 128), F32)], axis=1)
            dtail_ref[slot, WINDOW:] = row_split(sink_row, (EXTRA, width))


def gather_kernel(in_ref, out_ref):
    total = in_ref[0, :WINDOW].astype(F32)
    sink_row = row_join(in_ref[0, WINDOW:])
    for slot in range(1, in_ref.shape[0]):
        total = total + in_ref[slot, :WINDOW].astype(F32)
        sink_row = sink_row + row_join(in_ref[slot, WINDOW:])
    out_ref[:WINDOW] = total.astype(BF16)
    out_ref[WINDOW:] = row_split(sink_row, (EXTRA, in_ref.shape[2]))


def land_kernel(tok_count, blocks, table, here_ref, *refs):
    tok = lax.axis_index("tok")
    *in_refs, out_ref, sink_ref = refs
    state = [
        child_tail(table, tok, distance, tok_count, blocks) for distance in range(1, LAG + 1)
    ]
    out_ref[...] = jnp.zeros_like(out_ref)
    sink_row = row_join(here_ref[WINDOW:])
    for (valid, place), in_ref in zip(state, in_refs):
        sink_row = sink_row + row_join(in_ref[WINDOW:])

        @pl.when(valid)
        def _(place=place, in_ref=in_ref):
            total = out_ref[place].astype(F32) + in_ref[:WINDOW].astype(F32)
            out_ref[place] = total.astype(BF16)

    sink_ref[...] = jnp.broadcast_to(sink_row[:, :128], sink_ref.shape)


def total_kernel(
    dk_ref, dv_ref, halo_ref, tail_ref, sink_ref, far_ref, key_ref, value_ref, sink_grad
):
    rows = dk_ref.shape[0]
    slots, width = tail_ref.shape[0], tail_ref.shape[2] // 2
    halo_k = jnp.concatenate([halo_ref[pair][:, :128] for pair in range(PAIRS)], axis=1)
    halo_v = jnp.concatenate([halo_ref[pair][:, 128:] for pair in range(PAIRS)], axis=1)
    for in_ref, halo, at, out_ref in (
        (dk_ref, halo_k, 0, key_ref),
        (dv_ref, halo_v, width, value_ref),
    ):
        for begin in range(0, rows, WINDOW):
            here = slice(begin, begin + WINDOW)
            tails = [tail_ref[slot, here, at : at + width] for slot in range(slots)]
            total = in_ref[here, :] + jnp.concatenate(tails, axis=1).astype(F32)
            if begin == rows - WINDOW:
                total = total + halo.astype(F32)
            out_ref[here, :] = total.astype(BF16)
    sink_row = -(sink_ref[0:1] + far_ref[0:1])
    for head in range(sink_grad.shape[0]):
        sink_grad[head] = sink_row[0, head]


def local(
    queries, key_states, value_states, out_grad, sink_logits, branch_start, branch_len, parent_list
):
    tok_count, head_count = lax.axis_size("tok"), lax.axis_size("head")
    rows = queries.shape[0]
    blocks_here = rows // WINDOW
    blocks = blocks_here * head_count
    per_slot = KV_HEADS // head_count
    width = 2 * per_slot * HEAD_DIM

    def shape(dims, kind=BF16):
        return jax.ShapeDtypeStruct(dims, kind)

    table = jnp.concatenate([branch_start, branch_len, parent_list[:, 0], parent_list[:, 1]])
    slots, halo_out = pl.pallas_call(
        pack_kernel,
        out_shape=(shape((head_count, rows + EXTRA, width)), shape((PAIRS, WINDOW, 256))),
        in_specs=[SMEM, VMEM, VMEM],
        out_specs=(VMEM, VMEM),
        compiler_params=PARAMS,
        name="pack",
    )(sink_logits, key_states, value_states)
    halo = shift(halo_out, "head", 1)
    spread = lax.all_to_all(slots, "head", split_axis=0, concat_axis=0, tiled=True)
    *chosen, sinks = pl.pallas_call(
        functools.partial(choose_kernel, tok_count, blocks),
        out_shape=(shape((WINDOW, width)),) * LAG + (shape((KV_HEADS * GROUP, 128), F32),),
        in_specs=[SMEM, VMEM],
        out_specs=(VMEM,) * (LAG + 1),
        compiler_params=PARAMS,
        name="choose",
    )(table, spread)
    arrived = [shift(chosen[s - 1], "tok", s) for s in range(1, LAG + 1)]
    quarter = pl.pallas_call(
        functools.partial(arrive_kernel, tok_count),
        out_shape=shape((WINDOW, width)),
        in_specs=[SMEM] + [VMEM] * LAG,
        out_specs=VMEM,
        compiler_params=PARAMS,
        name="arrive",
    )(table, *arrived)
    tail = lax.all_gather(quarter, "head")
    slots_per_pair = 2 // per_slot
    big = pl.BlockSpec((WINDOW, 1024), lambda p, b: (b, p))
    small = pl.BlockSpec((rows, 128), lambda p, b: (0, p))
    near = pl.BlockSpec((1, WINDOW, 256), lambda p, b: (p, 0, 0))
    attended, query_grad, dk, dv, dhalo, dtail = pl.pallas_call(
        functools.partial(attend_kernel, tok_count, per_slot, blocks_here),
        grid=(PAIRS, blocks_here),
        out_shape=(
            shape(queries.shape),
            shape(queries.shape),
            shape(key_states.shape, F32),
            shape(key_states.shape, F32),
            shape((PAIRS, WINDOW, 256)),
            shape((head_count, WINDOW + EXTRA, width)),
        ),
        in_specs=[
            SMEM,
            pl.BlockSpec((2 * GROUP, 128), lambda p, b: (p, 0)),
            big,
            big,
            small,
            small,
            near,
            pl.BlockSpec((slots_per_pair, WINDOW, width), lambda p, b: (p, 0, 0)),
        ],
        out_specs=(
            big,
            big,
            small,
            small,
            near,
            pl.BlockSpec((slots_per_pair, WINDOW + EXTRA, width), lambda p, b: (p, 0, 0)),
        ),
        scratch_shapes=[
            pltpu.VMEM((WINDOW, 256), F32),
            pltpu.VMEM((2 * GROUP, WINDOW), F32),
            pltpu.VMEM((HEAD_DIM, 2048), BF16),
            pltpu.VMEM((HEAD_DIM, 2048), BF16),
            pltpu.VMEM((2 * WINDOW, 2048), BF16),
            pltpu.VMEM((2 * WINDOW, 2048), BF16),
        ],
        compiler_params=PARAMS,
        name="attend",
    )(table, sinks, queries, out_grad, key_states, value_states, halo, tail)
    halo_back = shift(dhalo, "head", -1)
    parts = lax.all_to_all(dtail, "head", split_axis=0, concat_axis=0, tiled=True)
    quarter_grad = pl.pallas_call(
        gather_kernel,
        out_shape=shape((WINDOW + EXTRA, width)),
        in_specs=[VMEM],
        out_specs=VMEM,
        compiler_params=PARAMS,
        name="gather",
    )(parts)
    returned = [ring(quarter_grad, "tok", -s) for s in range(1, LAG + 1)]
    landed, sink_near = pl.pallas_call(
        functools.partial(land_kernel, tok_count, blocks),
        out_shape=(shape((blocks, WINDOW, width)), shape((8, 128), F32)),
        in_specs=[SMEM] + [VMEM] * (LAG + 1),
        out_specs=(VMEM, VMEM),
        compiler_params=PARAMS,
        name="land",
    )(table, quarter_grad, *returned)
    tails_back = lax.all_to_all(
        landed.reshape(head_count, rows, width), "head", split_axis=0, concat_axis=0, tiled=True
    )
    span = LAG + 1
    while 2 * span < tok_count:
        sink_near = sink_near + ring(sink_near, "tok", -span)
        span *= 2
    sink_far = ring(sink_near, "tok", -span)
    key_grad, value_grad, sink_grad = pl.pallas_call(
        total_kernel,
        out_shape=(
            shape(key_states.shape),
            shape(value_states.shape),
            shape(sink_logits.shape, F32),
        ),
        in_specs=[VMEM] * 6,
        out_specs=(VMEM, VMEM, SMEM),
        compiler_params=PARAMS,
        name="total",
    )(dk, dv, halo_back, tails_back, sink_near, sink_far)
    return attended, query_grad, key_grad, value_grad, sink_grad


def solution(mesh):
    rows = P(("tok", "head"), None)
    return jax.shard_map(
        local,
        mesh=mesh,
        in_specs=(rows, rows, rows, rows, P("head"), P(), P(), P()),
        out_specs=(rows, rows, rows, rows, P("head")),
        check_vma=False,
    )
```

profile of v0, /device:TPU:3, one launch (start us, length us, event | category | flops | bytes accessed | tf_op | source)
XLA Modules:
  0.0 97.2 jit_solution(9274033161032251166)
XLA Ops:
  0.6 0.9 copy-done.2
  1.6 0.9 copy-done.4
  3.8 0.8 copy-done.6
  5.3 4.1 %all-to-all-start = ((bf16[4,272,256]{2,1,0:T(8,128)(2,1)}), bf16[4,272,256]{2,1,0:T(8,128)(2,1)S(1)}, u32[]{:S(2)}, u32[]{:S(2)}) async-start(bf16[4,272,256]{2,1,0:T(8,128)(2,1)} %copy-done.6), calls=%async_computation | async-start | bytes 1114112 | tf_op jit(solution)/shard_map/all_to_all | solution.py:381
  9.4 3.5 %collective-permute-start = (bf16[4,128,256]{2,1,0:T(8,128)(2,1)}, bf16[4,128,256]{2,1,0:T(8,128)(2,1)S(1)}, u32[]{:S(2)}, u32[]{:S(2)}) collective-permute-start(bf16[4,128,256]{2,1,0:T(8,128)(2,1)} %copy-done.10), channel_id=1, source_target_pairs={{0,1},{1,2},{2,3},{4,5},{5,6},{6,7},{8,9},{9,10},{10,11},{12,13},{... | collective-permute-start | bytes 786440 | tf_op jit(solution)/shard_map/ppermute | solution.py:31
  14.5 3.3 %all-to-all-done.all_ref = bf16[4,272,256]{2,1,0:T(8,128)(2,1)S(1)} async-done(((bf16[4,272,256]{2,1,0:T(8,128)(2,1)}), bf16[4,272,256]{2,1,0:T(8,128)(2,1)S(1)}, u32[]{:S(2)}, u32[]{:S(2)}) %all-to-all-start) | async-done | bytes 557088 | tf_op jit(solution)/shard_map/all_to_all | solution.py:381
  18.4 3.2 %collective-permute-start.1 = (bf16[128,256]{1,0:T(8,128)(2,1)S(1)}, bf16[128,256]{1,0:T(8,128)(2,1)S(1)}, u32[]{:S(2)}, u32[]{:S(2)}) collective-permute-start(bf16[128,256]{1,0:T(8,128)(2,1)S(1)} %get-tuple-element.25), channel_id=1, source_target_pairs={{0,4},{4,8},{8,12},{12,16},{16,20},{20,24},{24,28},{1,5},{5,9},{9,... | collective-permute-start | bytes 196616 | tf_op jit(solution)/shard_map/ppermute | solution.py:31
  21.6 3.2 %collective-permute-start.2 = (bf16[128,256]{1,0:T(8,128)(2,1)S(1)}, bf16[128,256]{1,0:T(8,128)(2,1)S(1)}, u32[]{:S(2)}, u32[]{:S(2)}) collective-permute-start(bf16[128,256]{1,0:T(8,128)(2,1)S(1)} %get-tuple-element.26), channel_id=1, source_target_pairs={{0,8},{4,12},{8,16},{12,20},{16,24},{20,28},{1,9},{5,13},{9,17},{1... | collective-permute-start | bytes 196616 | tf_op jit(solution)/shard_map/ppermute | solution.py:31
  24.8 4.1 %collective-permute-start.3 = (bf16[128,256]{1,0:T(8,128)(2,1)S(1)}, bf16[128,256]{1,0:T(8,128)(2,1)S(1)}, u32[]{:S(2)}, u32[]{:S(2)}) collective-permute-start(bf16[128,256]{1,0:T(8,128)(2,1)S(1)} %get-tuple-element.27), channel_id=1, source_target_pairs={{0,12},{4,16},{8,20},{12,24},{16,28},{1,13},{5,17},{9,21},{13,25},... | collective-permute-start | bytes 196616 | tf_op jit(solution)/shard_map/ppermute | solution.py:31
  29.0 1.3 %collective-permute-done.3.refs_2_ = bf16[128,256]{1,0:T(8,128)(2,1)S(1)} collective-permute-done((bf16[128,256]{1,0:T(8,128)(2,1)S(1)}, bf16[128,256]{1,0:T(8,128)(2,1)S(1)}, u32[]{:S(2)}, u32[]{:S(2)}) %collective-permute-start.3) | collective-permute-done | bytes 65568 | tf_op jit(solution)/shard_map/ppermute | solution.py:31
  30.8 7.9 %all-gather = bf16[512,256]{1,0:T(8,128)(2,1)S(1)} all-gather(bf16[128,256]{1,0:T(8,128)(2,1)S(1)} %arrive.1), channel_id=2, replica_groups=mesh['tok'=8,'head'=4] {'head'}, dimensions={0}, use_global_device_ids=true | all-gather | bytes 327680 | tf_op jit(solution)/shard_map/all_gather | solution.py:399
  38.8 1.6 %copy-done.1 = bf16[256,4096]{1,0:T(8,128)(2,1)S(1)} copy-done((bf16[256,4096]{1,0:T(8,128)(2,1)S(1)}, bf16[256,4096]{1,0:T(8,128)(2,1)}, u32[]{:S(2)}) %copy-start.1) | copy-done | bytes 2097176
  40.4 12.8 %attend.1 = (bf16[256,4096]{1,0:T(8,128)(2,1)}, bf16[256,4096]{1,0:T(8,128)(2,1)}, f32[256,512]{1,0:T(8,128)S(1)}, f32[256,512]{1,0:T(8,128)S(1)}, bf16[4,128,25...) custom-call(s32[64]{0:T(128)S(1)} %pad_add_fusion.table, f32[64,128]{1,0:T(8,128)S(1)} %get-tuple-element.23.sink_ref, ...), custom_call_target="tpu_custom_call" | custom-call | tf_op jit(solution)/shard_map/attend/pallas_call | solution.py:404
  53.2 13.9 %all_to_all.15.in_ref = bf16[4,144,256]{2,1,0:T(8,128)(2,1)S(1)} all-to-all(bf16[4,144,256]{2,1,0:T(8,128)(2,1)S(1)} %get-tuple-element.33), channel_id=1, replica_groups=mesh['tok'=8,'head'=4] {'head'}, dimensions={0} | all-to-all | bytes 589824 | tf_op jit(solution)/shard_map/all_to_all | solution.py:445
  67.1 3.5 %collective-permute-start.7 = (bf16[144,256]{1,0:T(8,128)(2,1)S(1)}, bf16[144,256]{1,0:T(8,128)(2,1)S(1)}, u32[]{:S(2)}, u32[]{:S(2)}) collective-permute-start(bf16[144,256]{1,0:T(8,128)(2,1)S(1)} %gather.1.here_ref), channel_id=1, source_target_pairs={{0,20},{4,24},{8,28},{12,0},{16,4},{20,8},{24,12},{28,16},{1,21},{... | collective-permute-start | bytes 221192 | tf_op jit(solution)/shard_map/ppermute | solution.py:36
  70.6 2.4 %collective-permute-start.6 = (bf16[144,256]{1,0:T(8,128)(2,1)S(1)}, bf16[144,256]{1,0:T(8,128)(2,1)S(1)}, u32[]{:S(2)}, u32[]{:S(2)}) collective-permute-start(bf16[144,256]{1,0:T(8,128)(2,1)S(1)} %gather.1.here_ref), channel_id=1, source_target_pairs={{0,24},{4,28},{8,0},{12,4},{16,8},{20,12},{24,16},{28,20},{1,25},{... | collective-permute-start | bytes 221192 | tf_op jit(solution)/shard_map/ppermute | solution.py:36
  73.0 2.3 %collective-permute-done.7.refs_2_ = bf16[144,256]{1,0:T(8,128)(2,1)S(1)} collective-permute-done((bf16[144,256]{1,0:T(8,128)(2,1)S(1)}, bf16[144,256]{1,0:T(8,128)(2,1)S(1)}, u32[]{:S(2)}, u32[]{:S(2)}) %collective-permute-start.7) | collective-permute-done | bytes 73760 | tf_op jit(solution)/shard_map/ppermute | solution.py:36
  75.3 1.8 %collective-permute-done.5.refs_0_ = bf16[144,256]{1,0:T(8,128)(2,1)S(1)} collective-permute-done((bf16[144,256]{1,0:T(8,128)(2,1)S(1)}, bf16[144,256]{1,0:T(8,128)(2,1)S(1)}, u32[]{:S(2)}, u32[]{:S(2)}) %collective-permute-start.5) | collective-permute-done | bytes 73760 | tf_op jit(solution)/shard_map/ppermute | solution.py:36
  77.1 1.4 %land.1 = (bf16[8,128,256]{2,1,0:T(8,128)(2,1)}, f32[8,128]{1,0:T(8,128)S(1)}) custom-call(s32[64]{0:T(128)S(1)} %pad_add_fusion.table, bf16[144,256]{1,0:T(8,128)(2,1)S(1)} %gather.1.here_ref, bf16[144,256]{1,0:T(8,128)(2,1)S(1)} %collective-permute-done.5.refs_0_, bf16[144,256]{1,0:T(8,128)(2,1)S(1)} %collective-permute-done.6.refs_1_, ...), custom_call_target="tpu_custom_call" | custom-call | tf_op jit(solution)/shard_map/land/pallas_call | solution.py:455
  78.5 5.7 %all-to-all-start.2 = ((bf16[4,256,256]{2,1,0:T(8,128)(2,1)}), bf16[4,256,256]{2,1,0:T(8,128)(2,1)S(1)}, u32[]{:S(2)}, u32[]{:S(2)}) async-start(bf16[4,256,256]{2,1,0:T(8,128)(2,1)} %bitcast.3), calls=%async_computation.2 | async-start | bytes 1048576 | tf_op jit(solution)/shard_map/all_to_all | solution.py:463
  84.2 1.9 %collective-permute-start.4 = (bf16[4,128,256]{2,1,0:T(8,128)(2,1)}, bf16[4,128,256]{2,1,0:T(8,128)(2,1)S(1)}, u32[]{:S(2)}, u32[]{:S(2)}) collective-permute-start(bf16[4,128,256]{2,1,0:T(8,128)(2,1)} %copy-done.11), channel_id=1, source_target_pairs={{1,0},{2,1},{3,2},{5,4},{6,5},{7,6},{9,8},{10,9},{11,10},{13,12},{... | collective-permute-start | bytes 786440 | tf_op jit(solution)/shard_map/ppermute | solution.py:31
  86.2 8.9 %collective-permute-done.4.halo_ref = bf16[4,128,256]{2,1,0:T(8,128)(2,1)S(1)} collective-permute-done((bf16[4,128,256]{2,1,0:T(8,128)(2,1)}, bf16[4,128,256]{2,1,0:T(8,128)(2,1)S(1)}, u32[]{:S(2)}, u32[]{:S(2)}) %collective-permute-start.4) | collective-permute-done | bytes 262176 | tf_op jit(solution)/shard_map/ppermute | solution.py:31
  95.2 1.0 %copy-done.8 = f32[256,512]{1,0:T(8,128)S(1)} copy-done((f32[256,512]{1,0:T(8,128)S(1)}, f32[256,512]{1,0:T(8,128)}, u32[]{:S(2)}) %copy-start.8) | copy-done | bytes 524312
  96.2 1.0 total.1
  (33 shorter events, 4.9 us)
Async XLA Ops:
  0.6 1.0 copy-start.2
  1.6 0.9 copy-start.4
  2.5 0.7 copy-start.9
  3.2 35.6 %copy-start = (bf16[256,4096]{1,0:T(8,128)(2,1)S(1)}, bf16[256,4096]{1,0:T(8,128)(2,1)}, u32[]{:S(2)}) copy-start(bf16[256,4096]{1,0:T(8,128)(2,1)} %q_ref.1) | copy-start | bytes 6291460
  3.2 35.6 %copy-start.3 = (bf16[256,512]{1,0:T(8,128)(2,1)S(1)}, bf16[256,512]{1,0:T(8,128)(2,1)}, u32[]{:S(2)}) copy-start(bf16[256,512]{1,0:T(8,128)(2,1)} %k_ref.1) | copy-start | bytes 786436
  3.2 35.6 %copy-start.5 = (bf16[256,512]{1,0:T(8,128)(2,1)S(1)}, bf16[256,512]{1,0:T(8,128)(2,1)}, u32[]{:S(2)}) copy-start(bf16[256,512]{1,0:T(8,128)(2,1)} %v_ref.1) | copy-start | bytes 786436
  3.8 0.8 copy-start.6
  4.6 0.7 copy-start.10
  5.3 12.4 %all-to-all-start = ((bf16[4,272,256]{2,1,0:T(8,128)(2,1)}), bf16[4,272,256]{2,1,0:T(8,128)(2,1)S(1)}, u32[]{:S(2)}, u32[]{:S(2)}) async-start(bf16[4,272,256]{2,1,0:T(8,128)(2,1)} %copy-done.6), calls=%async_computation | async-start | bytes 1114112 | tf_op jit(solution)/shard_map/all_to_all | solution.py:381
  9.4 29.3 %collective-permute-start = (bf16[4,128,256]{2,1,0:T(8,128)(2,1)}, bf16[4,128,256]{2,1,0:T(8,128)(2,1)S(1)}, u32[]{:S(2)}, u32[]{:S(2)}) collective-permute-start(bf16[4,128,256]{2,1,0:T(8,128)(2,1)} %copy-done.10), channel_id=1, source_target_pairs={{0,1},{1,2},{2,3},{4,5},{5,6},{6,7},{8,9},{9,10},{10,11},{12,13},{... | collective-permute-start | bytes 786440 | tf_op jit(solution)/shard_map/ppermute | solution.py:31
  18.4 10.5 %collective-permute-start.1 = (bf16[128,256]{1,0:T(8,128)(2,1)S(1)}, bf16[128,256]{1,0:T(8,128)(2,1)S(1)}, u32[]{:S(2)}, u32[]{:S(2)}) collective-permute-start(bf16[128,256]{1,0:T(8,128)(2,1)S(1)} %get-tuple-element.25), channel_id=1, source_target_pairs={{0,4},{4,8},{8,12},{12,16},{16,20},{20,24},{24,28},{1,5},{5,9},{9,... | collective-permute-start | bytes 196616 | tf_op jit(solution)/shard_map/ppermute | solution.py:31
  21.6 7.4 %collective-permute-start.2 = (bf16[128,256]{1,0:T(8,128)(2,1)S(1)}, bf16[128,256]{1,0:T(8,128)(2,1)S(1)}, u32[]{:S(2)}, u32[]{:S(2)}) collective-permute-start(bf16[128,256]{1,0:T(8,128)(2,1)S(1)} %get-tuple-element.26), channel_id=1, source_target_pairs={{0,8},{4,12},{8,16},{12,20},{16,24},{20,28},{1,9},{5,13},{9,17},{1... | collective-permute-start | bytes 196616 | tf_op jit(solution)/shard_map/ppermute | solution.py:31
  24.8 5.5 %collective-permute-start.3 = (bf16[128,256]{1,0:T(8,128)(2,1)S(1)}, bf16[128,256]{1,0:T(8,128)(2,1)S(1)}, u32[]{:S(2)}, u32[]{:S(2)}) collective-permute-start(bf16[128,256]{1,0:T(8,128)(2,1)S(1)} %get-tuple-element.27), channel_id=1, source_target_pairs={{0,12},{4,16},{8,20},{12,24},{16,28},{1,13},{5,17},{9,21},{13,25},... | collective-permute-start | bytes 196616 | tf_op jit(solution)/shard_map/ppermute | solution.py:31
  38.8 1.6 %copy-start.1 = (bf16[256,4096]{1,0:T(8,128)(2,1)S(1)}, bf16[256,4096]{1,0:T(8,128)(2,1)}, u32[]{:S(2)}) copy-start(bf16[256,4096]{1,0:T(8,128)(2,1)} %g_ref.1) | copy-start | bytes 6291460
  53.1 14.0 %copy-start.7 = (f32[256,512]{1,0:T(8,128)}, f32[256,512]{1,0:T(8,128)S(1)}, u32[]{:S(2)}) copy-start(f32[256,512]{1,0:T(8,128)S(1)} %get-tuple-element.31.dv_ref) | copy-start | bytes 1572868
  53.2 25.4 %copy-start.11 = (bf16[4,128,256]{2,1,0:T(8,128)(2,1)}, bf16[4,128,256]{2,1,0:T(8,128)(2,1)S(1)}, u32[]{:S(2)}) copy-start(bf16[4,128,256]{2,1,0:T(8,128)(2,1)S(1)} %get-tuple-element.32) | copy-start | bytes 786436
  67.1 8.2 %collective-permute-start.7 = (bf16[144,256]{1,0:T(8,128)(2,1)S(1)}, bf16[144,256]{1,0:T(8,128)(2,1)S(1)}, u32[]{:S(2)}, u32[]{:S(2)}) collective-permute-start(bf16[144,256]{1,0:T(8,128)(2,1)S(1)} %gather.1.here_ref), channel_id=1, source_target_pairs={{0,20},{4,24},{8,28},{12,0},{16,4},{20,8},{24,12},{28,16},{1,21},{... | collective-permute-start | bytes 221192 | tf_op jit(solution)/shard_map/ppermute | solution.py:36
  70.6 4.7 %collective-permute-start.6 = (bf16[144,256]{1,0:T(8,128)(2,1)S(1)}, bf16[144,256]{1,0:T(8,128)(2,1)S(1)}, u32[]{:S(2)}, u32[]{:S(2)}) collective-permute-start(bf16[144,256]{1,0:T(8,128)(2,1)S(1)} %gather.1.here_ref), channel_id=1, source_target_pairs={{0,24},{4,28},{8,0},{12,4},{16,8},{20,12},{24,16},{28,20},{1,25},{... | collective-permute-start | bytes 221192 | tf_op jit(solution)/shard_map/ppermute | solution.py:36
  73.0 4.2 %collective-permute-start.5 = (bf16[144,256]{1,0:T(8,128)(2,1)S(1)}, bf16[144,256]{1,0:T(8,128)(2,1)S(1)}, u32[]{:S(2)}, u32[]{:S(2)}) collective-permute-start(bf16[144,256]{1,0:T(8,128)(2,1)S(1)} %gather.1.here_ref), channel_id=1, source_target_pairs={{0,28},{4,0},{8,4},{12,8},{16,12},{20,16},{24,20},{28,24},{1,29},{... | collective-permute-start | bytes 221192 | tf_op jit(solution)/shard_map/ppermute | solution.py:36
  78.5 16.6 %all-to-all-start.2 = ((bf16[4,256,256]{2,1,0:T(8,128)(2,1)}), bf16[4,256,256]{2,1,0:T(8,128)(2,1)S(1)}, u32[]{:S(2)}, u32[]{:S(2)}) async-start(bf16[4,256,256]{2,1,0:T(8,128)(2,1)} %bitcast.3), calls=%async_computation.2 | async-start | bytes 1048576 | tf_op jit(solution)/shard_map/all_to_all | solution.py:463
  84.2 11.0 %collective-permute-start.4 = (bf16[4,128,256]{2,1,0:T(8,128)(2,1)}, bf16[4,128,256]{2,1,0:T(8,128)(2,1)S(1)}, u32[]{:S(2)}, u32[]{:S(2)}) collective-permute-start(bf16[4,128,256]{2,1,0:T(8,128)(2,1)} %copy-done.11), channel_id=1, source_target_pairs={{1,0},{2,1},{3,2},{5,4},{6,5},{7,6},{9,8},{10,9},{11,10},{13,12},{... | collective-permute-start | bytes 786440 | tf_op jit(solution)/shard_map/ppermute | solution.py:31
  86.2 9.0 %collective-permute-start.8 = (f32[8,128]{1,0:T(8,128)S(1)}, f32[8,128]{1,0:T(8,128)S(1)}, u32[]{:S(2)}, u32[]{:S(2)}) collective-permute-start(f32[8,128]{1,0:T(8,128)S(1)} %get-tuple-element.35.sink_ref), channel_id=1, source_target_pairs={{0,16},{4,20},{8,24},{12,28},{16,0},{20,4},{24,8},{28,12},{1,17},{... | collective-permute-start | bytes 12296 | tf_op jit(solution)/shard_map/ppermute | solution.py:36
  95.2 1.0 %copy-start.8 = (f32[256,512]{1,0:T(8,128)S(1)}, f32[256,512]{1,0:T(8,128)}, u32[]{:S(2)}) copy-start(f32[256,512]{1,0:T(8,128)} %copy-done.7) | copy-start | bytes 1572868
where the time goes:
time: 97.7 us; the launch traced here: 97.2 us
  starting transfers between devices  31.7 us (32%)
  blocking collectives  21.8 us (22%)
  waiting for transfers between devices  17.7 us (18%)
  Pallas kernels  17 us (17%)
  local copies, waits for them, and re-layouts  7.45 us (8%)
    ppermute x5, starting transfers between devices, shift(): lax.ppermute(value, axis, [(source, source + steps) for source in range(l...  16 us
    all_to_all x1, blocking collectives, local(): lax.all_to_all(dtail, 'head', split_axis=0, concat_axis=0, tiled=True)  13.9 us
    pallas_call x1, Pallas kernels, local(): pl.pallas_call(functools.partial(attend_kernel, tok_count, per_slot, bloc...  12.8 us
    ppermute x5, waiting for transfers between devices, shift(): lax.ppermute(value, axis, [(source, source + steps) for source in range(l...  10.2 us
    all_gather x1, blocking collectives, local(): tail = lax.all_gather(quarter, 'head')  7.91 us
    unnamed x24, local copies, waits for them, and re-layouts  6.69 us
    ppermute x4, starting transfers between devices, ring(): lax.ppermute(value, axis, [(source, (source + steps) % count) for source...  5.91 us
    all_to_all x1, starting transfers between devices, local(): lax.all_to_all(landed.reshape(head_count, rows, width), 'head', split_axi...  5.66 us
  transfers between devices with their start and end apart: 11, of which 5 were waited for; matrix products, arithmetic and copies ran while one was open for 2% of the time, Pallas kernels for 1%

commit v1 on v0

--- a/solution.py
+++ b/solution.py
@@ -22,6 +22,7 @@
 
 SMEM = pl.BlockSpec(memory_space=pltpu.SMEM)
 VMEM = pl.BlockSpec(memory_space=pltpu.VMEM)
+HBM = pl.BlockSpec(memory_space=pltpu.HBM)
 PARAMS = pltpu.CompilerParams(vmem_limit_bytes=24 * 1024 * 1024)
 
 
@@ -73,39 +74,69 @@
     return alive, opening, jnp.logical_not(opening) | has_tail
 
 
-def pack_kernel(sinks, key_ref, value_ref, slot_ref, halo_ref):
-    slots, rows = slot_ref.shape[0], key_ref.shape[0]
+def take(ref, slot, width):
+    if width % 128 == 0:
+        return ref[:, pl.ds(pl.multiple_of(slot * width, width), width)]
+    value = ref[:, :width]
+    for other in range(1, ref.shape[1] // width):
+        value = jnp.where(slot == other, ref[:, other * width : (other + 1) * width], value)
+    return value
+
+
+def pack_kernel(sink_hbm, key_hbm, value_hbm, *refs):
+    *slot_refs, halo_ref, sinks, keys, values, sems = refs
+    copies = [
+        pltpu.make_async_copy(source, target, sems.at[place])
+        for place, (source, target) in enumerate(
+            ((sink_hbm, sinks), (key_hbm, keys), (value_hbm, values))
+        )
+    ]
+    for copy in copies:
+        copy.start()
+    for copy in copies:
+        copy.wait()
+    slots, rows = len(slot_refs), keys.shape[0]
+    head = lax.axis_index("head")
     width = KV_HEADS * HEAD_DIM // slots
     lane = lax.broadcasted_iota(jnp.int32, (1, 2 * width), 1)
     sink_row = jnp.zeros((1, 2 * width), F32)
-    for head in range(sinks.shape[0]):
-        sink_row = jnp.where(lane == head, sinks[head], sink_row)
+    for place in range(sinks.shape[0]):
+        sink_row = jnp.where(lane == place, sinks[place], sink_row)
     extra = row_split(sink_row, (EXTRA, 2 * width))
-    for slot in range(slots):
-        lanes = slice(slot * width, (slot + 1) * width)
-        slot_ref[slot, :rows] = jnp.concatenate([key_ref[:, lanes], value_ref[:, lanes]], axis=1)
-        slot_ref[slot, rows:] = extra
+    for step, slot_ref in enumerate(slot_refs):
+        slot = lax.rem(head + step, slots)
+        slot_ref[:rows] = jnp.concatenate(
+            [take(keys, slot, width), take(values, slot, width)], axis=1
+        )
+        slot_ref[rows:] = extra
     for pair in range(PAIRS):
         lanes = slice(pair * 128, (pair + 1) * 128)
         last = slice(rows - WINDOW, rows)
-        halo_ref[pair] = jnp.concatenate([key_ref[last, lanes], value_ref[last, lanes]], axis=1)
-
-
-def choose_kernel(tok_count, blocks, table, all_ref, *refs):
-    tok = lax.axis_index("tok")
-    *out_refs, sink_ref = refs
-    slots = all_ref.shape[0]
-    rows = all_ref.shape[1] - EXTRA
+        halo_ref[pair] = jnp.concatenate([keys[last, lanes], values[last, lanes]], axis=1)
+
+
+def choose_kernel(tok_count, blocks, table, *refs):
+    slots = len(refs) - LAG - 1
+    slot_refs, out_refs, sink_ref = refs[:slots], refs[slots:-1], refs[-1]
+    tok, head = lax.axis_index("tok"), lax.axis_index("head")
+    rows = slot_refs[0].shape[0] - EXTRA
     blocks_here = rows // WINDOW
     heads = sink_ref.shape[0] // slots
     for distance, out_ref in enumerate(out_refs, 1):
         _, place = child_tail(table, tok, distance, tok_count, blocks)
         begin = pl.multiple_of(place % blocks_here * WINDOW, WINDOW)
-        out_ref[...] = all_ref[place // blocks_here, pl.ds(begin, WINDOW), :]
-    for slot in range(slots):
-        sink_row = row_join(all_ref[slot, rows:, :])[:, :128]
+        wanted = lax.rem(head - place // blocks_here + slots, slots)
+        for step, slot_ref in enumerate(slot_refs):
+
+            @pl.when(wanted == step)
+            def _(out_ref=out_ref, slot_ref=slot_ref, begin=begin):
+                out_ref[...] = slot_ref[pl.ds(begin, WINDOW), :]
+
+    for step, slot_ref in enumerate(slot_refs):
+        source = lax.rem(head - step + slots, slots)
+        sink_row = row_join(slot_ref[rows:, :])[:, :128]
         turned = jnp.broadcast_to(sink_row, (128, 128)).T
-        sink_ref[slot * heads : (slot + 1) * heads, :] = turned[:heads]
+        sink_ref[pl.ds(pl.multiple_of(source * heads, heads), heads), :] = turned[:heads]
 
 
 def arrive_kernel(tok_count, table, *refs):
@@ -122,8 +153,8 @@
 
 def attend_kernel(
     tok_count,
-    per_slot,
     blocks_here,
+    slots,
     table,
     sink_ref,
     q_ref,
@@ -131,20 +162,13 @@
     k_ref,
     v_ref,
     halo_ref,
-    tail_ref,
-    o_ref,
-    dq_ref,
-    dk_ref,
-    dv_ref,
-    dhalo_ref,
-    dtail_ref,
-    tail_sum,
-    sink_rows,
-    q_turned,
-    g_turned,
-    prob2,
-    slope2,
+    *refs,
 ):
+    tail_refs, refs = refs[:slots], refs[slots:]
+    o_ref, dq_ref, dk_ref, dv_ref, dhalo_ref = refs[:5]
+    dtail_refs, refs = refs[5 : 5 + slots], refs[5 + slots :]
+    tails, tail_sum, sink_rows, q_turned, g_turned, prob2, slope2 = refs
+    per_slot = KV_HEADS // slots
     pair, block = pl.program_id(0), pl.program_id(1)
     tok, head = lax.axis_index("tok"), lax.axis_index("head")
     number = (tok * lax.axis_size("head") + head) * blocks_here + block
@@ -153,6 +177,11 @@
     before = pl.ds(pl.multiple_of(jnp.maximum(block - 1, 0) * WINDOW, WINDOW), WINDOW)
     first = block == 0
 
+    @pl.when(first & (pair == 0))
+    def _():
+        for step, tail_ref in enumerate(tail_refs):
+            tails[lax.rem(head - step + slots, slots)] = tail_ref[...]
+
     @pl.when(first)
     def _():
         tail_sum[...] = jnp.zeros_like(tail_sum)
@@ -170,11 +199,12 @@
     def _():
         halo = halo_ref[0]
         if per_slot == 2:
-            tail = tail_ref[0]
+            tail = tails[pair]
             tail_k, tail_v = tail[:, :128], tail[:, 128:]
         else:
-            tail_k = jnp.concatenate([tail_ref[0][:, :64], tail_ref[1][:, :64]], axis=1)
-            tail_v = jnp.concatenate([tail_ref[0][:, 64:], tail_ref[1][:, 64:]], axis=1)
+            tail_a, tail_b = tails[2 * pair], tails[2 * pair + 1]
+            tail_k = jnp.concatenate([tail_a[:, :64], tail_b[:, :64]], axis=1)
+            tail_v = jnp.concatenate([tail_a[:, 64:], tail_b[:, 64:]], axis=1)
         near_k = jnp.where(first, halo[:, :128], k_ref[before, :])
         near_v = jnp.where(first, halo[:, 128:], v_ref[before, :])
         prev_k = jnp.where(opening, tail_k, near_k)
@@ -287,56 +317,67 @@
 
     @pl.when(block == blocks_here - 1)
     def _():
-        slots, width = dtail_ref.shape[0], dtail_ref.shape[2]
-        heads = 2 * GROUP // slots
+        width = dtail_refs[0].shape[1]
+        heads = per_slot * GROUP
         total = tail_sum[...].astype(BF16)
-        for slot in range(slots):
-            feats = slice(slot * width // 2, (slot + 1) * width // 2)
-            dtail_ref[slot, :WINDOW] = jnp.concatenate(
-                [total[:, :128][:, feats], total[:, 128:][:, feats]], axis=1
-            )
-            rows = sink_rows[slot * heads : (slot + 1) * heads]
+        for part in range(2 // per_slot):
+            feats = slice(part * width // 2, (part + 1) * width // 2)
+            tail = jnp.concatenate([total[:, :128][:, feats], total[:, 128:][:, feats]], axis=1)
+            rows = sink_rows[part * heads : (part + 1) * heads]
             rows = jnp.concatenate([rows, jnp.zeros((128 - heads, WINDOW), F32)], axis=0)
             sink_row = jnp.sum(rows.T, axis=0, keepdims=True)
             if width > 128:
                 sink_row = jnp.concatenate([sink_row, jnp.zeros((1, width - 128), F32)], axis=1)
-            dtail_ref[slot, WINDOW:] = row_split(sink_row, (EXTRA, width))
-
-
-def gather_kernel(in_ref, out_ref):
-    total = in_ref[0, :WINDOW].astype(F32)
-    sink_row = row_join(in_ref[0, WINDOW:])
-    for slot in range(1, in_ref.shape[0]):
-        total = total + in_ref[slot, :WINDOW].astype(F32)
-        sink_row = sink_row + row_join(in_ref[slot, WINDOW:])
+            extra = row_split(sink_row, (EXTRA, width))
+            wanted = lax.rem(pair * (2 // per_slot) + part - head + slots, slots)
+            for step, dtail_ref in enumerate(dtail_refs):
+
+                @pl.when(wanted == step)
+                def _(dtail_ref=dtail_ref, tail=tail, extra=extra):
+                    dtail_ref[:WINDOW] = tail
+                    dtail_ref[WINDOW:] = extra
+
+
+def gather_kernel(*refs):
+    *in_refs, out_ref = refs
+    total, sink_row = 0.0, 0.0
+    for in_ref in in_refs:
+        total = total + in_ref[:WINDOW].astype(F32)
+        sink_row = sink_row + row_join(in_ref[WINDOW:])
     out_ref[:WINDOW] = total.astype(BF16)
-    out_ref[WINDOW:] = row_split(sink_row, (EXTRA, in_ref.shape[2]))
+    out_ref[WINDOW:] = row_split(sink_row, (EXTRA, out_ref.shape[1]))
 
 
 def land_kernel(tok_count, blocks, table, here_ref, *refs):
-    tok = lax.axis_index("tok")
-    *in_refs, out_ref, sink_ref = refs
-    state = [
-        child_tail(table, tok, distance, tok_count, blocks) for distance in range(1, LAG + 1)
-    ]
-    out_ref[...] = jnp.zeros_like(out_ref)
+    tok, head = lax.axis_index("tok"), lax.axis_index("head")
+    in_refs, out_refs, sink_ref = refs[:LAG], refs[LAG:-1], refs[-1]
+    slots = len(out_refs)
+    blocks_here = blocks // slots
+    for out_ref in out_refs:
+        out_ref[...] = jnp.zeros_like(out_ref)
     sink_row = row_join(here_ref[WINDOW:])
-    for (valid, place), in_ref in zip(state, in_refs):
+    for distance, in_ref in enumerate(in_refs, 1):
+        valid, place = child_tail(table, tok, distance, tok_count, blocks)
         sink_row = sink_row + row_join(in_ref[WINDOW:])
-
-        @pl.when(valid)
-        def _(place=place, in_ref=in_ref):
-            total = out_ref[place].astype(F32) + in_ref[:WINDOW].astype(F32)
-            out_ref[place] = total.astype(BF16)
+        wanted = lax.rem(place // blocks_here - head + slots, slots)
+        here = pl.ds(pl.multiple_of(place % blocks_here * WINDOW, WINDOW), WINDOW)
+        for step, out_ref in enumerate(out_refs):
+
+            @pl.when(valid & (wanted == step))
+            def _(out_ref=out_ref, in_ref=in_ref, here=here):
+                total = out_ref[here, :].astype(F32) + in_ref[:WINDOW].astype(F32)
+                out_ref[here, :] = total.astype(BF16)
 
     sink_ref[...] = jnp.broadcast_to(sink_row[:, :128], sink_ref.shape)
 
 
-def total_kernel(
-    dk_ref, dv_ref, halo_ref, tail_ref, sink_ref, far_ref, key_ref, value_ref, sink_grad
-):
-    rows = dk_ref.shape[0]
-    slots, width = tail_ref.shape[0], tail_ref.shape[2] // 2
+def total_kernel(dk_ref, dv_ref, halo_ref, sink_ref, far_ref, *refs):
+    *tail_refs, key_ref, value_ref, sink_grad, tails = refs
+    slots, rows = len(tail_refs), dk_ref.shape[0]
+    width = tails.shape[2] // 2
+    head = lax.axis_index("head")
+    for step, tail_ref in enumerate(tail_refs):
+        tails[lax.rem(head - step + slots, slots)] = tail_ref[...]
     halo_k = jnp.concatenate([halo_ref[pair][:, :128] for pair in range(PAIRS)], axis=1)
     halo_v = jnp.concatenate([halo_ref[pair][:, 128:] for pair in range(PAIRS)], axis=1)
     for in_ref, halo, at, out_ref in (
@@ -345,14 +386,18 @@
     ):
         for begin in range(0, rows, WINDOW):
             here = slice(begin, begin + WINDOW)
-            tails = [tail_ref[slot, here, at : at + width] for slot in range(slots)]
-            total = in_ref[here, :] + jnp.concatenate(tails, axis=1).astype(F32)
+            parts = [tails[slot, here, at : at + width] for slot in range(slots)]
+            total = in_ref[here, :] + jnp.concatenate(parts, axis=1).astype(F32)
             if begin == rows - WINDOW:
                 total = total + halo.astype(F32)
             out_ref[here, :] = total.astype(BF16)
     sink_row = -(sink_ref[0:1] + far_ref[0:1])
-    for head in range(sink_grad.shape[0]):
-        sink_grad[head] = sink_row[0, head]
+    for place in range(sink_grad.shape[0]):
+        sink_grad[place] = sink_row[0, place]
+
+
+def swap(values, axis):
+    return [values[0]] + [ring(values[step], axis, step) for step in range(1, len(values))]
 
 
 def local(
@@ -369,25 +414,32 @@
         return jax.ShapeDtypeStruct(dims, kind)
 
     table = jnp.concatenate([branch_start, branch_len, parent_list[:, 0], parent_list[:, 1]])
-    slots, halo_out = pl.pallas_call(
+    *slots, halo_out = pl.pallas_call(
         pack_kernel,
-        out_shape=(shape((head_count, rows + EXTRA, width)), shape((PAIRS, WINDOW, 256))),
-        in_specs=[SMEM, VMEM, VMEM],
-        out_specs=(VMEM, VMEM),
+        out_shape=(shape((rows + EXTRA, width)),) * head_count + (shape((PAIRS, WINDOW, 256)),),
+        in_specs=[HBM] * 3,
+        out_specs=(VMEM,) * (head_count + 1),
+        scratch_shapes=[
+            pltpu.SMEM(sink_logits.shape, F32),
+            pltpu.VMEM(key_states.shape, BF16),
+            pltpu.VMEM(key_states.shape, BF16),
+            pltpu.SemaphoreType.DMA((3,)),
+        ],
         compiler_params=PARAMS,
         name="pack",
     )(sink_logits, key_states, value_states)
-    halo = shift(halo_out, "head", 1)
-    spread = lax.all_to_all(slots, "head", split_axis=0, concat_axis=0, tiled=True)
+    spread = swap(slots, "head")
     *chosen, sinks = pl.pallas_call(
         functools.partial(choose_kernel, tok_count, blocks),
         out_shape=(shape((WINDOW, width)),) * LAG + (shape((KV_HEADS * GROUP, 128), F32),),
-        in_specs=[SMEM, VMEM],
+        in_specs=[SMEM] + [VMEM] * head_count,
         out_specs=(VMEM,) * (LAG + 1),
         compiler_params=PARAMS,
         name="choose",
-    )(table, spread)
-    arrived = [shift(chosen[s - 1], "tok", s) for s in range(1, LAG + 1)]
+    )(table, *spread)
+    arrived = [shift(chosen[s - 1], "tok", s) for s in range(LAG, 0, -1)][::-1]
+    halo_out, _ = lax.optimization_barrier((halo_out, chosen[0]))
+    halo = shift(halo_out, "head", 1)
     quarter = pl.pallas_call(
         functools.partial(arrive_kernel, tok_count),
         out_shape=shape((WINDOW, width)),
@@ -396,13 +448,14 @@
         compiler_params=PARAMS,
         name="arrive",
     )(table, *arrived)
-    tail = lax.all_gather(quarter, "head")
-    slots_per_pair = 2 // per_slot
+    tails = swap([quarter] * head_count, "head")
     big = pl.BlockSpec((WINDOW, 1024), lambda p, b: (b, p))
     small = pl.BlockSpec((rows, 128), lambda p, b: (0, p))
     near = pl.BlockSpec((1, WINDOW, 256), lambda p, b: (p, 0, 0))
-    attended, query_grad, dk, dv, dhalo, dtail = pl.pallas_call(
-        functools.partial(attend_kernel, tok_count, per_slot, blocks_here),
+    whole = pl.BlockSpec((WINDOW, width), lambda p, b: (0, 0))
+    whole_back = pl.BlockSpec((WINDOW + EXTRA, width), lambda p, b: (0, 0))
+    attended, query_grad, dk, dv, dhalo, *dtail = pl.pallas_call(
+        functools.partial(attend_kernel, tok_count, blocks_here, head_count),
         grid=(PAIRS, blocks_here),
         out_shape=(
             shape(queries.shape),
@@ -410,8 +463,8 @@
             shape(key_states.shape, F32),
             shape(key_states.shape, F32),
             shape((PAIRS, WINDOW, 256)),
-            shape((head_count, WINDOW + EXTRA, width)),
-        ),
+        )
+        + (shape((WINDOW + EXTRA, width)),) * head_count,
         in_specs=[
             SMEM,
             pl.BlockSpec((2 * GROUP, 128), lambda p, b: (p, 0)),
@@ -420,17 +473,11 @@
             small,
             small,
             near,
-            pl.BlockSpec((slots_per_pair, WINDOW, width), lambda p, b: (p, 0, 0)),
-        ],
-        out_specs=(
-            big,
-            big,
-            small,
-            small,
-            near,
-            pl.BlockSpec((slots_per_pair, WINDOW + EXTRA, width), lambda p, b: (p, 0, 0)),
-        ),
+        ]
+        + [whole] * head_count,
+        out_specs=(big, big, small, small, near) + (whole_back,) * head_count,
         scratch_shapes=[
+            pltpu.VMEM((head_count, WINDOW, width), BF16),
             pltpu.VMEM((WINDOW, 256), F32),
             pltpu.VMEM((2 * GROUP, WINDOW), F32),
             pltpu.VMEM((HEAD_DIM, 2048), BF16),
@@ -440,29 +487,28 @@
         ],
         compiler_params=PARAMS,
         name="attend",
-    )(table, sinks, queries, out_grad, key_states, value_states, halo, tail)
-    halo_back = shift(dhalo, "head", -1)
-    parts = lax.all_to_all(dtail, "head", split_axis=0, concat_axis=0, tiled=True)
+    )(table, sinks, queries, out_grad, key_states, value_states, halo, *tails)
+    parts = swap(dtail, "head")
     quarter_grad = pl.pallas_call(
         gather_kernel,
         out_shape=shape((WINDOW + EXTRA, width)),
-        in_specs=[VMEM],
+        in_specs=[VMEM] * head_count,
         out_specs=VMEM,
         compiler_params=PARAMS,
         name="gather",
-    )(parts)
-    returned = [ring(quarter_grad, "tok", -s) for s in range(1, LAG + 1)]
-    landed, sink_near = pl.pallas_call(
+    )(*parts)
+    returned = [ring(quarter_grad, "tok", -s) for s in range(LAG, 0, -1)][::-1]
+    dhalo, _ = lax.optimization_barrier((dhalo, quarter_grad))
+    halo_back = shift(dhalo, "head", -1)
+    *landed, sink_near = pl.pallas_call(
         functools.partial(land_kernel, tok_count, blocks),
-        out_shape=(shape((blocks, WINDOW, width)), shape((8, 128), F32)),
+        out_shape=(shape((rows, width)),) * head_count + (shape((8, 128), F32),),
         in_specs=[SMEM] + [VMEM] * (LAG + 1),
-        out_specs=(VMEM, VMEM),
+        out_specs=(VMEM,) * (head_count + 1),
         compiler_params=PARAMS,
         name="land",
     )(table, quarter_grad, *returned)
-    tails_back = lax.all_to_all(
-        landed.reshape(head_count, rows, width), "head", split_axis=0, concat_axis=0, tiled=True
-    )
+    tails_back = swap(landed, "head")
     span = LAG + 1
     while 2 * span < tok_count:
         sink_near = sink_near + ring(sink_near, "tok", -span)
@@ -475,11 +521,12 @@
             shape(value_states.shape),
             shape(sink_logits.shape, F32),
         ),
-        in_specs=[VMEM] * 6,
+        in_specs=[VMEM] * (5 + head_count),
         out_specs=(VMEM, VMEM, SMEM),
+        scratch_shapes=[pltpu.VMEM((head_count, rows, width), BF16)],
         compiler_params=PARAMS,
         name="total",
-    )(dk, dv, halo_back, tails_back, sink_near, sink_far)
+    )(dk, dv, halo_back, sink_near, sink_far, *tails_back)
     return attended, query_grad, key_grad, value_grad, sink_grad
 
 

time: 97.7 us -> 87.8 us (0.90)
  blocking collectives: 21.8 us -> 0 us
  Pallas kernels: 17 us -> 23.1 us
  waiting for transfers between devices: 17.7 us -> 23.4 us
  starting transfers between devices: 31.7 us -> 30.2 us
    ppermute x4 -> x16, waiting for transfers between devices: 4.16 us -> 21.5 us  [ring(): lax.ppermute(value, axis, [(source, (source + steps) % count) for source...]
    all_to_all x1 -> x0, blocking collectives: 13.9 us -> none  [local(): lax.all_to_all(dtail, 'head', split_axis=0, concat_axis=0, tiled=True)]
    ppermute x4 -> x16, starting transfers between devices: 5.91 us -> 15.8 us  [ring(): lax.ppermute(value, axis, [(source, (source + steps) % count) for source...]
    all_to_all x2 -> x0, starting transfers between devices: 9.78 us -> none  [the longest x1 5.66 us: local(): lax.all_to_all(landed.reshape(head_count, rows, width), 'head', split_axi...]
    ppermute x5, waiting for transfers between devices: 10.2 us -> 1.87 us  [shift(): lax.ppermute(value, axis, [(source, source + steps) for source in range(l...]
    all_gather x1 -> x0, blocking collectives: 7.91 us -> none  [local(): tail = lax.all_gather(quarter, 'head')]
    pallas_call x2, Pallas kernels: 13.4 us -> 19.9 us  [the longest x1 19.3 us: local(): pl.pallas_call(functools.partial(attend_kernel, tok_count, blocks_here, h...]
    all_to_all x2 -> x0, waiting for transfers between devices: 3.29 us -> none  [the longest x1 3.28 us: local(): lax.all_to_all(slots, 'head', split_axis=0, concat_axis=0, tiled=True)]
  transfers between devices with their start and end apart: 11 -> 21, of which waited for: 5 -> 14; matrix products, arithmetic and copies ran while one was open for 2% -> 2% of each run, Pallas kernels for 1% -> 1%
where the time goes in v1:
time: 87.8 us; the launch traced here: 86.5 us
  starting transfers between devices  30.2 us (34%)
  waiting for transfers between devices  23.4 us (27%)
  Pallas kernels  23.1 us (26%)
  local copies, waits for them, and re-layouts  8.39 us (10%)
    ppermute x16, waiting for transfers between devices, ring(): lax.ppermute(value, axis, [(source, (source + steps) % count) for source...  21.5 us
    pallas_call x1, Pallas kernels, local(): pl.pallas_call(functools.partial(attend_kernel, tok_count, blocks_here, h...  19.3 us
    ppermute x16, starting transfers between devices, ring(): lax.ppermute(value, axis, [(source, (source + steps) % count) for source...  15.8 us
    ppermute x5, starting transfers between devices, shift(): lax.ppermute(value, axis, [(source, source + steps) for source in range(l...  14.4 us
    unnamed x14, local copies, waits for them, and re-layouts  7.63 us
    ppermute x5, waiting for transfers between devices, shift(): lax.ppermute(value, axis, [(source, source + steps) for source in range(l...  1.87 us
  transfers between devices with their start and end apart: 21, of which 14 were waited for; matrix products, arithmetic and copies ran while one was open for 2% of the time, Pallas kernels for 1%

profile of v1, /device:TPU:3, one launch (start us, length us, event | category | flops | bytes accessed | tf_op | source)
XLA Modules:
  0.0 86.5 jit_solution(9668731034506699159)
XLA Ops:
  3.9 1.9 %collective-permute-start = (bf16[272,256]{1,0:T(8,128)(2,1)S(1)}, bf16[272,256]{1,0:T(8,128)(2,1)S(1)}, u32[]{:S(2)}, u32[]{:S(2)}) collective-permute-start(bf16[272,256]{1,0:T(8,128)(2,1)S(1)} %get-tuple-element.34), channel_id=1, source_target_pairs={{0,1},{1,2},{2,3},{3,0},{4,5},{5,6},{6,7},{7,4},{8,9},{9,10},{10,1... | collective-permute-start | bytes 417800 | tf_op jit(solution)/shard_map/ppermute | solution.py:37
  8.6 3.6 %collective-permute-done.1.refs_2_ = bf16[272,256]{1,0:T(8,128)(2,1)S(1)} collective-permute-done((bf16[272,256]{1,0:T(8,128)(2,1)S(1)}, bf16[272,256]{1,0:T(8,128)(2,1)S(1)}, u32[]{:S(2)}, u32[]{:S(2)}) %collective-permute-start.1) | collective-permute-done | bytes 139296 | tf_op jit(solution)/shard_map/ppermute | solution.py:37
  13.7 1.9 %collective-permute-start.3 = (bf16[4,128,256]{2,1,0:T(8,128)(2,1)S(1)}, bf16[4,128,256]{2,1,0:T(8,128)(2,1)S(1)}, u32[]{:S(2)}, u32[]{:S(2)}) collective-permute-start(bf16[4,128,256]{2,1,0:T(8,128)(2,1)S(1)} %get-tuple-element.40), channel_id=1, source_target_pairs={{0,1},{1,2},{2,3},{4,5},{5,6},{6,7},{8,9},{9,10},{10,11},{12,13},{... | collective-permute-start | bytes 786440 | tf_op jit(solution)/shard_map/ppermute | solution.py:32
  15.6 3.2 %collective-permute-start.5 = (bf16[128,256]{1,0:T(8,128)(2,1)S(1)}, bf16[128,256]{1,0:T(8,128)(2,1)S(1)}, u32[]{:S(2)}, u32[]{:S(2)}) collective-permute-start(bf16[128,256]{1,0:T(8,128)(2,1)S(1)} %get-tuple-element.41), channel_id=1, source_target_pairs={{0,8},{4,12},{8,16},{12,20},{16,24},{20,28},{1,9},{5,13},{9,17},{1... | collective-permute-start | bytes 196616 | tf_op jit(solution)/shard_map/ppermute | solution.py:32
  18.8 4.2 %collective-permute-start.6 = (bf16[128,256]{1,0:T(8,128)(2,1)S(1)}, bf16[128,256]{1,0:T(8,128)(2,1)S(1)}, u32[]{:S(2)}, u32[]{:S(2)}) collective-permute-start(bf16[128,256]{1,0:T(8,128)(2,1)S(1)} %get-tuple-element.42), channel_id=1, source_target_pairs={{0,12},{4,16},{8,20},{12,24},{16,28},{1,13},{5,17},{9,21},{13,25},... | collective-permute-start | bytes 196616 | tf_op jit(solution)/shard_map/ppermute | solution.py:32
  23.0 3.1 %collective-permute-start.4 = (bf16[128,256]{1,0:T(8,128)(2,1)S(1)}, bf16[128,256]{1,0:T(8,128)(2,1)S(1)}, u32[]{:S(2)}, u32[]{:S(2)}) collective-permute-start(bf16[128,256]{1,0:T(8,128)(2,1)S(1)} %get-tuple-element.39), channel_id=1, source_target_pairs={{0,4},{4,8},{8,12},{12,16},{16,20},{20,24},{24,28},{1,5},{5,9},{9,... | collective-permute-start | bytes 196616 | tf_op jit(solution)/shard_map/ppermute | solution.py:32
  26.2 1.9 %collective-permute-done.4.refs_0_ = bf16[128,256]{1,0:T(8,128)(2,1)S(1)} collective-permute-done((bf16[128,256]{1,0:T(8,128)(2,1)S(1)}, bf16[128,256]{1,0:T(8,128)(2,1)S(1)}, u32[]{:S(2)}, u32[]{:S(2)}) %collective-permute-start.4) | collective-permute-done | bytes 65568 | tf_op jit(solution)/shard_map/ppermute | solution.py:32
  28.6 2.3 %collective-permute-start.9 = (bf16[128,256]{1,0:T(8,128)(2,1)S(1)}, bf16[128,256]{1,0:T(8,128)(2,1)S(1)}, u32[]{:S(2)}, u32[]{:S(2)}) collective-permute-start(bf16[128,256]{1,0:T(8,128)(2,1)S(1)} %arrive.1.refs_0_), channel_id=1, source_target_pairs={{0,3},{1,0},{2,1},{3,2},{4,7},{5,4},{6,5},{7,6},{8,11},{9,8},{10,9... | collective-permute-start | bytes 196616 | tf_op jit(solution)/shard_map/ppermute | solution.py:37
  30.9 1.2 %collective-permute-start.8 = (bf16[128,256]{1,0:T(8,128)(2,1)S(1)}, bf16[128,256]{1,0:T(8,128)(2,1)S(1)}, u32[]{:S(2)}, u32[]{:S(2)}) collective-permute-start(bf16[128,256]{1,0:T(8,128)(2,1)S(1)} %arrive.1.refs_0_), channel_id=1, source_target_pairs={{0,2},{1,3},{2,0},{3,1},{4,6},{5,7},{6,4},{7,5},{8,10},{9,11},{10,... | collective-permute-start | bytes 196616 | tf_op jit(solution)/shard_map/ppermute | solution.py:37
  32.6 2.0 %collective-permute-done.9.refs_3_ = bf16[128,256]{1,0:T(8,128)(2,1)S(1)} collective-permute-done((bf16[128,256]{1,0:T(8,128)(2,1)S(1)}, bf16[128,256]{1,0:T(8,128)(2,1)S(1)}, u32[]{:S(2)}, u32[]{:S(2)}) %collective-permute-start.9) | collective-permute-done | bytes 65568 | tf_op jit(solution)/shard_map/ppermute | solution.py:37
  35.0 1.6 %copy-done = bf16[256,4096]{1,0:T(8,128)(2,1)S(1)} copy-done((bf16[256,4096]{1,0:T(8,128)(2,1)S(1)}, bf16[256,4096]{1,0:T(8,128)(2,1)}, u32[]{:S(2)}) %copy-start) | copy-done | bytes 2097176
  36.6 1.6 %copy-done.1 = bf16[256,4096]{1,0:T(8,128)(2,1)S(1)} copy-done((bf16[256,4096]{1,0:T(8,128)(2,1)S(1)}, bf16[256,4096]{1,0:T(8,128)(2,1)}, u32[]{:S(2)}) %copy-start.1) | copy-done | bytes 2097176
  40.1 19.3 %attend.1 = (bf16[256,4096]{1,0:T(8,128)(2,1)}, bf16[256,4096]{1,0:T(8,128)(2,1)}, f32[256,512]{1,0:T(8,128)S(1)}, f32[256,512]{1,0:T(8,128)S(1)}, bf16[4,128,25...) custom-call(s32[64]{0:T(128)S(1)} %pad_add_fusion.table, ...), custom_call_target="tpu_custom_call" | custom-call | tf_op jit(solution)/shard_map/attend/pallas_call | solution.py:457
  59.3 2.2 %collective-permute-start.10 = (bf16[144,256]{1,0:T(8,128)(2,1)S(1)}, bf16[144,256]{1,0:T(8,128)(2,1)S(1)}, u32[]{:S(2)}, u32[]{:S(2)}) collective-permute-start(bf16[144,256]{1,0:T(8,128)(2,1)S(1)} %get-tuple-element.49), channel_id=1, source_target_pairs={{0,1},{1,2},{2,3},{3,0},{4,5},{5,6},{6,7},{7,4},{8,9},{9,10},{10,1... | collective-permute-start | bytes 221192 | tf_op jit(solution)/shard_map/ppermute | solution.py:37
  63.0 3.0 %collective-permute-done.11.refs_2_ = bf16[144,256]{1,0:T(8,128)(2,1)S(1)} collective-permute-done((bf16[144,256]{1,0:T(8,128)(2,1)S(1)}, bf16[144,256]{1,0:T(8,128)(2,1)S(1)}, u32[]{:S(2)}, u32[]{:S(2)}) %collective-permute-start.11) | collective-permute-done | bytes 73760 | tf_op jit(solution)/shard_map/ppermute | solution.py:37
  66.6 1.9 %collective-permute-start.13 = (bf16[4,128,256]{2,1,0:T(8,128)(2,1)S(1)}, bf16[4,128,256]{2,1,0:T(8,128)(2,1)S(1)}, u32[]{:S(2)}, u32[]{:S(2)}) collective-permute-start(bf16[4,128,256]{2,1,0:T(8,128)(2,1)S(1)} %get-tuple-element.52), channel_id=1, source_target_pairs={{1,0},{2,1},{3,2},{5,4},{6,5},{7,6},{9,8},{10,9},{11,10},{13,12},{... | collective-permute-start | bytes 786440 | tf_op jit(solution)/shard_map/ppermute | solution.py:32
  68.6 1.2 %collective-permute-start.15 = (bf16[144,256]{1,0:T(8,128)(2,1)S(1)}, bf16[144,256]{1,0:T(8,128)(2,1)S(1)}, u32[]{:S(2)}, u32[]{:S(2)}) collective-permute-start(bf16[144,256]{1,0:T(8,128)(2,1)S(1)} %gather.1.here_ref), channel_id=1, source_target_pairs={{0,24},{4,28},{8,0},{12,4},{16,8},{20,12},{24,16},{28,20},{1,25},{... | collective-permute-start | bytes 221192 | tf_op jit(solution)/shard_map/ppermute | solution.py:37
  69.8 1.8 %collective-permute-start.14 = (bf16[144,256]{1,0:T(8,128)(2,1)S(1)}, bf16[144,256]{1,0:T(8,128)(2,1)S(1)}, u32[]{:S(2)}, u32[]{:S(2)}) collective-permute-start(bf16[144,256]{1,0:T(8,128)(2,1)S(1)} %gather.1.here_ref), channel_id=1, source_target_pairs={{0,28},{4,0},{8,4},{12,8},{16,12},{20,16},{24,20},{28,24},{1,29},{... | collective-permute-start | bytes 221192 | tf_op jit(solution)/shard_map/ppermute | solution.py:37
  71.6 3.6 %collective-permute-done.16.refs_2_ = bf16[144,256]{1,0:T(8,128)(2,1)S(1)} collective-permute-done((bf16[144,256]{1,0:T(8,128)(2,1)S(1)}, bf16[144,256]{1,0:T(8,128)(2,1)S(1)}, u32[]{:S(2)}, u32[]{:S(2)}) %collective-permute-start.16) | collective-permute-done | bytes 73760 | tf_op jit(solution)/shard_map/ppermute | solution.py:37
  76.9 1.8 %collective-permute-start.18 = (bf16[256,256]{1,0:T(8,128)(2,1)S(1)}, bf16[256,256]{1,0:T(8,128)(2,1)S(1)}, u32[]{:S(2)}, u32[]{:S(2)}) collective-permute-start(bf16[256,256]{1,0:T(8,128)(2,1)S(1)} %get-tuple-element.55), channel_id=1, source_target_pairs={{0,1},{1,2},{2,3},{3,0},{4,5},{5,6},{6,7},{7,4},{8,9},{9,10},{10,1... | collective-permute-start | bytes 393224 | tf_op jit(solution)/shard_map/ppermute | solution.py:37
  79.1 1.2 %collective-permute-start.17 = (f32[8,128]{1,0:T(8,128)S(1)}, f32[8,128]{1,0:T(8,128)S(1)}, u32[]{:S(2)}, u32[]{:S(2)}) collective-permute-start(f32[8,128]{1,0:T(8,128)S(1)} %get-tuple-element.53.sink_ref), channel_id=1, source_target_pairs={{0,16},{4,20},{8,24},{12,28},{16,0},{20,4},{24,8},{28,12},{1,17},{... | collective-permute-start | bytes 12296 | tf_op jit(solution)/shard_map/ppermute | solution.py:37
  80.3 2.2 %collective-permute-done.17.far_ref = f32[8,128]{1,0:T(8,128)S(1)} collective-permute-done((f32[8,128]{1,0:T(8,128)S(1)}, f32[8,128]{1,0:T(8,128)S(1)}, u32[]{:S(2)}, u32[]{:S(2)}) %collective-permute-start.17) | collective-permute-done | bytes 4128 | tf_op jit(solution)/shard_map/ppermute | solution.py:37
  82.5 2.4 %collective-permute-done.19.refs_2_ = bf16[256,256]{1,0:T(8,128)(2,1)S(1)} collective-permute-done((bf16[256,256]{1,0:T(8,128)(2,1)S(1)}, bf16[256,256]{1,0:T(8,128)(2,1)S(1)}, u32[]{:S(2)}, u32[]{:S(2)}) %collective-permute-start.19) | collective-permute-done | bytes 131104 | tf_op jit(solution)/shard_map/ppermute | solution.py:37
  85.5 1.0 %total.1 = (bf16[256,512]{1,0:T(8,128)(2,1)}, bf16[256,512]{1,0:T(8,128)(2,1)}, f32[16]{0:T(128)}) custom-call(f32[256,512]{1,0:T(8,128)S(1)} %get-tuple-element.45.dk_ref, f32[256,512]{1,0:T(8,128)S(1)} %get-tuple-element.46.dv_ref, bf16[4,128,256]{2,1,0:T(8,128)(2,1)S(1)} %collective-permute-done.13.halo_ref, f32[8,128]{1,0:T(8,128)S(1)} %get-tuple-element.53.sink_ref, ...), custom_call_target="tpu_custom_call" | custom-call | tf_op jit(solution)/shard_map/total/pallas_call | solution.py:517
  (41 shorter events, 15.7 us)
Async XLA Ops:
  0.6 1.0 %copy-start.2 = (bf16[256,512]{1,0:T(8,128)(2,1)S(1)}, bf16[256,512]{1,0:T(8,128)(2,1)}, u32[]{:S(2)}) copy-start(bf16[256,512]{1,0:T(8,128)(2,1)} %k_ref.1) | copy-start | bytes 786436
  3.9 4.7 %collective-permute-start = (bf16[272,256]{1,0:T(8,128)(2,1)S(1)}, bf16[272,256]{1,0:T(8,128)(2,1)S(1)}, u32[]{:S(2)}, u32[]{:S(2)}) collective-permute-start(bf16[272,256]{1,0:T(8,128)(2,1)S(1)} %get-tuple-element.34), channel_id=1, source_target_pairs={{0,1},{1,2},{2,3},{3,0},{4,5},{5,6},{6,7},{7,4},{8,9},{9,10},{10,1... | collective-permute-start | bytes 417800 | tf_op jit(solution)/shard_map/ppermute | solution.py:37
  5.7 6.5 %collective-permute-start.1 = (bf16[272,256]{1,0:T(8,128)(2,1)S(1)}, bf16[272,256]{1,0:T(8,128)(2,1)S(1)}, u32[]{:S(2)}, u32[]{:S(2)}) collective-permute-start(bf16[272,256]{1,0:T(8,128)(2,1)S(1)} %get-tuple-element.35), channel_id=1, source_target_pairs={{0,2},{1,3},{2,0},{3,1},{4,6},{5,7},{6,4},{7,5},{8,10},{9,11},{10,... | collective-permute-start | bytes 417800 | tf_op jit(solution)/shard_map/ppermute | solution.py:37
  6.0 6.9 %collective-permute-start.2 = (bf16[272,256]{1,0:T(8,128)(2,1)S(1)}, bf16[272,256]{1,0:T(8,128)(2,1)S(1)}, u32[]{:S(2)}, u32[]{:S(2)}) collective-permute-start(bf16[272,256]{1,0:T(8,128)(2,1)S(1)} %get-tuple-element.36), channel_id=1, source_target_pairs={{0,3},{1,0},{2,1},{3,2},{4,7},{5,4},{6,5},{7,6},{8,11},{9,8},{10,9... | collective-permute-start | bytes 417800 | tf_op jit(solution)/shard_map/ppermute | solution.py:37
  13.7 21.3 %collective-permute-start.3 = (bf16[4,128,256]{2,1,0:T(8,128)(2,1)S(1)}, bf16[4,128,256]{2,1,0:T(8,128)(2,1)S(1)}, u32[]{:S(2)}, u32[]{:S(2)}) collective-permute-start(bf16[4,128,256]{2,1,0:T(8,128)(2,1)S(1)} %get-tuple-element.40), channel_id=1, source_target_pairs={{0,1},{1,2},{2,3},{4,5},{5,6},{6,7},{8,9},{9,10},{10,11},{12,13},{... | collective-permute-start | bytes 786440 | tf_op jit(solution)/shard_map/ppermute | solution.py:32
  15.6 10.5 %collective-permute-start.5 = (bf16[128,256]{1,0:T(8,128)(2,1)S(1)}, bf16[128,256]{1,0:T(8,128)(2,1)S(1)}, u32[]{:S(2)}, u32[]{:S(2)}) collective-permute-start(bf16[128,256]{1,0:T(8,128)(2,1)S(1)} %get-tuple-element.41), channel_id=1, source_target_pairs={{0,8},{4,12},{8,16},{12,20},{16,24},{20,28},{1,9},{5,13},{9,17},{1... | collective-permute-start | bytes 196616 | tf_op jit(solution)/shard_map/ppermute | solution.py:32
  18.8 7.3 %collective-permute-start.6 = (bf16[128,256]{1,0:T(8,128)(2,1)S(1)}, bf16[128,256]{1,0:T(8,128)(2,1)S(1)}, u32[]{:S(2)}, u32[]{:S(2)}) collective-permute-start(bf16[128,256]{1,0:T(8,128)(2,1)S(1)} %get-tuple-element.42), channel_id=1, source_target_pairs={{0,12},{4,16},{8,20},{12,24},{16,28},{1,13},{5,17},{9,21},{13,25},... | collective-permute-start | bytes 196616 | tf_op jit(solution)/shard_map/ppermute | solution.py:32
  23.0 5.0 %collective-permute-start.4 = (bf16[128,256]{1,0:T(8,128)(2,1)S(1)}, bf16[128,256]{1,0:T(8,128)(2,1)S(1)}, u32[]{:S(2)}, u32[]{:S(2)}) collective-permute-start(bf16[128,256]{1,0:T(8,128)(2,1)S(1)} %get-tuple-element.39), channel_id=1, source_target_pairs={{0,4},{4,8},{8,12},{12,16},{16,20},{20,24},{24,28},{1,5},{5,9},{9,... | collective-permute-start | bytes 196616 | tf_op jit(solution)/shard_map/ppermute | solution.py:32
  28.6 6.0 %collective-permute-start.9 = (bf16[128,256]{1,0:T(8,128)(2,1)S(1)}, bf16[128,256]{1,0:T(8,128)(2,1)S(1)}, u32[]{:S(2)}, u32[]{:S(2)}) collective-permute-start(bf16[128,256]{1,0:T(8,128)(2,1)S(1)} %arrive.1.refs_0_), channel_id=1, source_target_pairs={{0,3},{1,0},{2,1},{3,2},{4,7},{5,4},{6,5},{7,6},{8,11},{9,8},{10,9... | collective-permute-start | bytes 196616 | tf_op jit(solution)/shard_map/ppermute | solution.py:37
  30.9 4.1 %collective-permute-start.8 = (bf16[128,256]{1,0:T(8,128)(2,1)S(1)}, bf16[128,256]{1,0:T(8,128)(2,1)S(1)}, u32[]{:S(2)}, u32[]{:S(2)}) collective-permute-start(bf16[128,256]{1,0:T(8,128)(2,1)S(1)} %arrive.1.refs_0_), channel_id=1, source_target_pairs={{0,2},{1,3},{2,0},{3,1},{4,6},{5,7},{6,4},{7,5},{8,10},{9,11},{10,... | collective-permute-start | bytes 196616 | tf_op jit(solution)/shard_map/ppermute | solution.py:37
  32.1 2.9 %collective-permute-start.7 = (bf16[128,256]{1,0:T(8,128)(2,1)S(1)}, bf16[128,256]{1,0:T(8,128)(2,1)S(1)}, u32[]{:S(2)}, u32[]{:S(2)}) collective-permute-start(bf16[128,256]{1,0:T(8,128)(2,1)S(1)} %arrive.1.refs_0_), channel_id=1, source_target_pairs={{0,1},{1,2},{2,3},{3,0},{4,5},{5,6},{6,7},{7,4},{8,9},{9,10},{10,1... | collective-permute-start | bytes 196616 | tf_op jit(solution)/shard_map/ppermute | solution.py:37
  35.0 1.6 %copy-start = (bf16[256,4096]{1,0:T(8,128)(2,1)S(1)}, bf16[256,4096]{1,0:T(8,128)(2,1)}, u32[]{:S(2)}) copy-start(bf16[256,4096]{1,0:T(8,128)(2,1)} %q_ref.1) | copy-start | bytes 6291460
  36.6 1.6 %copy-start.1 = (bf16[256,4096]{1,0:T(8,128)(2,1)S(1)}, bf16[256,4096]{1,0:T(8,128)(2,1)}, u32[]{:S(2)}) copy-start(bf16[256,4096]{1,0:T(8,128)(2,1)} %g_ref.1) | copy-start | bytes 6291460
  59.3 3.6 %collective-permute-start.10 = (bf16[144,256]{1,0:T(8,128)(2,1)S(1)}, bf16[144,256]{1,0:T(8,128)(2,1)S(1)}, u32[]{:S(2)}, u32[]{:S(2)}) collective-permute-start(bf16[144,256]{1,0:T(8,128)(2,1)S(1)} %get-tuple-element.49), channel_id=1, source_target_pairs={{0,1},{1,2},{2,3},{3,0},{4,5},{5,6},{6,7},{7,4},{8,9},{9,10},{10,1... | collective-permute-start | bytes 221192 | tf_op jit(solution)/shard_map/ppermute | solution.py:37
  61.6 4.4 %collective-permute-start.11 = (bf16[144,256]{1,0:T(8,128)(2,1)S(1)}, bf16[144,256]{1,0:T(8,128)(2,1)S(1)}, u32[]{:S(2)}, u32[]{:S(2)}) collective-permute-start(bf16[144,256]{1,0:T(8,128)(2,1)S(1)} %get-tuple-element.50), channel_id=1, source_target_pairs={{0,2},{1,3},{2,0},{3,1},{4,6},{5,7},{6,4},{7,5},{8,10},{9,11},{10,... | collective-permute-start | bytes 221192 | tf_op jit(solution)/shard_map/ppermute | solution.py:37
  62.4 4.1 %collective-permute-start.12 = (bf16[144,256]{1,0:T(8,128)(2,1)S(1)}, bf16[144,256]{1,0:T(8,128)(2,1)S(1)}, u32[]{:S(2)}, u32[]{:S(2)}) collective-permute-start(bf16[144,256]{1,0:T(8,128)(2,1)S(1)} %get-tuple-element.51), channel_id=1, source_target_pairs={{0,3},{1,0},{2,1},{3,2},{4,7},{5,4},{6,5},{7,6},{8,11},{9,8},{10,9... | collective-permute-start | bytes 221192 | tf_op jit(solution)/shard_map/ppermute | solution.py:37
  66.6 19.0 %collective-permute-start.13 = (bf16[4,128,256]{2,1,0:T(8,128)(2,1)S(1)}, bf16[4,128,256]{2,1,0:T(8,128)(2,1)S(1)}, u32[]{:S(2)}, u32[]{:S(2)}) collective-permute-start(bf16[4,128,256]{2,1,0:T(8,128)(2,1)S(1)} %get-tuple-element.52), channel_id=1, source_target_pairs={{1,0},{2,1},{3,2},{5,4},{6,5},{7,6},{9,8},{10,9},{11,10},{13,12},{... | collective-permute-start | bytes 786440 | tf_op jit(solution)/shard_map/ppermute | solution.py:32
  68.5 6.7 %collective-permute-start.16 = (bf16[144,256]{1,0:T(8,128)(2,1)S(1)}, bf16[144,256]{1,0:T(8,128)(2,1)S(1)}, u32[]{:S(2)}, u32[]{:S(2)}) collective-permute-start(bf16[144,256]{1,0:T(8,128)(2,1)S(1)} %gather.1.here_ref), channel_id=1, source_target_pairs={{0,20},{4,24},{8,28},{12,0},{16,4},{20,8},{24,12},{28,16},{1,21},{... | collective-permute-start | bytes 221192 | tf_op jit(solution)/shard_map/ppermute | solution.py:37
  68.6 6.6 %collective-permute-start.15 = (bf16[144,256]{1,0:T(8,128)(2,1)S(1)}, bf16[144,256]{1,0:T(8,128)(2,1)S(1)}, u32[]{:S(2)}, u32[]{:S(2)}) collective-permute-start(bf16[144,256]{1,0:T(8,128)(2,1)S(1)} %gather.1.here_ref), channel_id=1, source_target_pairs={{0,24},{4,28},{8,0},{12,4},{16,8},{20,12},{24,16},{28,20},{1,25},{... | collective-permute-start | bytes 221192 | tf_op jit(solution)/shard_map/ppermute | solution.py:37
  69.8 6.4 %collective-permute-start.14 = (bf16[144,256]{1,0:T(8,128)(2,1)S(1)}, bf16[144,256]{1,0:T(8,128)(2,1)S(1)}, u32[]{:S(2)}, u32[]{:S(2)}) collective-permute-start(bf16[144,256]{1,0:T(8,128)(2,1)S(1)} %gather.1.here_ref), channel_id=1, source_target_pairs={{0,28},{4,0},{8,4},{12,8},{16,12},{20,16},{24,20},{28,24},{1,29},{... | collective-permute-start | bytes 221192 | tf_op jit(solution)/shard_map/ppermute | solution.py:37
  76.9 5.6 %collective-permute-start.18 = (bf16[256,256]{1,0:T(8,128)(2,1)S(1)}, bf16[256,256]{1,0:T(8,128)(2,1)S(1)}, u32[]{:S(2)}, u32[]{:S(2)}) collective-permute-start(bf16[256,256]{1,0:T(8,128)(2,1)S(1)} %get-tuple-element.55), channel_id=1, source_target_pairs={{0,1},{1,2},{2,3},{3,0},{4,5},{5,6},{6,7},{7,4},{8,9},{9,10},{10,1... | collective-permute-start | bytes 393224 | tf_op jit(solution)/shard_map/ppermute | solution.py:37
  78.6 6.3 %collective-permute-start.19 = (bf16[256,256]{1,0:T(8,128)(2,1)S(1)}, bf16[256,256]{1,0:T(8,128)(2,1)S(1)}, u32[]{:S(2)}, u32[]{:S(2)}) collective-permute-start(bf16[256,256]{1,0:T(8,128)(2,1)S(1)} %get-tuple-element.56), channel_id=1, source_target_pairs={{0,2},{1,3},{2,0},{3,1},{4,6},{5,7},{6,4},{7,5},{8,10},{9,11},{10,... | collective-permute-start | bytes 393224 | tf_op jit(solution)/shard_map/ppermute | solution.py:37
  79.0 6.6 %collective-permute-start.20 = (bf16[256,256]{1,0:T(8,128)(2,1)S(1)}, bf16[256,256]{1,0:T(8,128)(2,1)S(1)}, u32[]{:S(2)}, u32[]{:S(2)}) collective-permute-start(bf16[256,256]{1,0:T(8,128)(2,1)S(1)} %get-tuple-element.57), channel_id=1, source_target_pairs={{0,3},{1,0},{2,1},{3,2},{4,7},{5,4},{6,5},{7,6},{8,11},{9,8},{10,9... | collective-permute-start | bytes 393224 | tf_op jit(solution)/shard_map/ppermute | solution.py:37
  79.1 3.4 %collective-permute-start.17 = (f32[8,128]{1,0:T(8,128)S(1)}, f32[8,128]{1,0:T(8,128)S(1)}, u32[]{:S(2)}, u32[]{:S(2)}) collective-permute-start(f32[8,128]{1,0:T(8,128)S(1)} %get-tuple-element.53.sink_ref), channel_id=1, source_target_pairs={{0,16},{4,20},{8,24},{12,28},{16,0},{20,4},{24,8},{28,12},{1,17},{... | collective-permute-start | bytes 12296 | tf_op jit(solution)/shard_map/ppermute | solution.py:37
  (4 other events, 3.5 us)

commit v2 on v1

--- a/solution.py
+++ b/solution.py
@@ -11,6 +11,7 @@
 KV_HEADS = 8
 GROUP = 8
 WINDOW = 128
+HALF = WINDOW // 2
 LAG = 3
 BR_DEV = 2
 PAIRS = KV_HEADS // 2
@@ -209,80 +210,127 @@
         near_v = jnp.where(first, halo[:, 128:], v_ref[before, :])
         prev_k = jnp.where(opening, tail_k, near_k)
         prev_v = jnp.where(opening, tail_v, near_v)
-        both_k = jnp.concatenate([k_ref[here, :], prev_k], axis=0) * BF16(FACTOR)
-        both_v = jnp.concatenate([v_ref[here, :], prev_v], axis=0)
-        turned_k, turned_v = both_k.T, both_v.T
+        own_k, own_v = k_ref[here, :], v_ref[here, :]
+
+        def halves(own, prev):
+            return (
+                jnp.concatenate([own[:HALF], prev[:HALF], prev[HALF:]], axis=0),
+                jnp.concatenate([own[HALF:], prev[HALF:], own[:HALF]], axis=0),
+            )
+
+        seen_k = halves(own_k * BF16(FACTOR), prev_k * BF16(FACTOR))
+        seen_v = halves(own_v, prev_v)
+        turned_k = tuple(value.T for value in seen_k)
+        turned_v = tuple(value.T for value in seen_v)
         bias = jnp.where(prev_ok, 0.0, LOW)
-        key_place = lax.broadcasted_iota(jnp.int32, (WINDOW, WINDOW), 0)
-        query_place = lax.broadcasted_iota(jnp.int32, (WINDOW, WINDOW), 1)
-        own_one = key_place <= query_place
-        own = jnp.concatenate([own_one, own_one], axis=1)
+        key_place = lax.broadcasted_iota(jnp.int32, (HALF, 4 * HALF), 0)
+        query_place = lax.broadcasted_iota(jnp.int32, (HALF, 4 * HALF), 1) & (HALF - 1)
+        own = key_place <= query_place
         own16 = own.astype(F32).astype(BF16)
+        left = lax.broadcasted_iota(jnp.int32, (1, 128), 1) < HALF
         turn = (((1,), (1,)), ((), ()))
-        couples = GROUP // 2
-
-        def columns(index):
-            return slice(index * 128, (index + 1) * 128)
+        items = [(unit, half, quad) for unit in range(2) for half in range(2) for quad in range(2)]
 
         def wide(index):
             return slice(index * 256, (index + 1) * 256)
 
         def feats(index):
-            unit = index // couples
+            unit = items[index][0]
             return slice(unit * HEAD_DIM, (unit + 1) * HEAD_DIM)
 
+        def corner(index):
+            unit, half, quad = items[index]
+            lane = unit * 512 + quad * 256
+            rows = slice(half * HALF, (half + 1) * HALF)
+            return rows, slice(lane, lane + 128), slice(lane + 128, lane + 256)
+
+        def turned(ref, index):
+            rows, left_lanes, right_lanes = corner(index)
+            tile = jnp.concatenate([ref[rows, left_lanes], ref[rows, right_lanes]], axis=0).T
+            return jnp.concatenate([tile[:64], tile[64:]], axis=1)
+
         def products(index):
-            q_t, g_t = q_ref[:, columns(index)].T, g_ref[:, columns(index)].T
-            q_t = jnp.concatenate([q_t[:64], q_t[64:]], axis=1)
-            g_t = jnp.concatenate([g_t[:64], g_t[64:]], axis=1)
+            half = items[index][1]
+            q_t, g_t = turned(q_ref, index), turned(g_ref, index)
             q_turned[:, wide(index)] = q_t
             g_turned[:, wide(index)] = g_t
-            score2 = jnp.dot(both_k[:, feats(index)], q_t, preferred_element_type=F32)
-            dp2 = jnp.dot(both_v[:, feats(index)], g_t, preferred_element_type=F32)
-            score = jnp.where(own, score2[:WINDOW], score2[WINDOW:] + bias)
-            return score, jnp.where(own, dp2[:WINDOW], dp2[WINDOW:])
-
-        def weigh(index, score, dp):
-            row = index * 2
-            sink = jnp.concatenate([sink_ref[row : row + 1], sink_ref[row + 1 : row + 2]], axis=1)
-            peak = jnp.maximum(jnp.max(score, axis=0, keepdims=True), sink)
-            weight = jnp.exp(score - peak)
+            score = jnp.dot(seen_k[half][:, feats(index)], q_t, preferred_element_type=F32)
+            dp = jnp.dot(seen_v[half][:, feats(index)], g_t, preferred_element_type=F32)
+            edge = jnp.where(own, score[:HALF], score[HALF : 2 * HALF] + bias)
+            whole = score[2 * HALF :] + bias if half == 0 else score[2 * HALF :]
+            dp_edge = jnp.where(own, dp[:HALF], dp[HALF : 2 * HALF])
+            return edge, whole, dp_edge, dp[2 * HALF :]
+
+        def weigh(index, edge, whole, dp_edge, dp_whole):
+            unit, half, quad = items[index]
+            row = unit * GROUP + quad * 4
+            sink = jnp.concatenate(
+                [
+                    jnp.where(left, sink_ref[row : row + 1], sink_ref[row + 2 : row + 3]),
+                    jnp.where(left, sink_ref[row + 1 : row + 2], sink_ref[row + 3 : row + 4]),
+                ],
+                axis=1,
+            )
+            peak = jnp.max(jnp.maximum(edge, whole), axis=0, keepdims=True)
+            peak = jnp.maximum(peak, sink)
+            edge, whole = jnp.exp(edge - peak), jnp.exp(whole - peak)
             sink_weight = jnp.exp(sink - peak)
-            inverse = 1.0 / (jnp.sum(weight, axis=0, keepdims=True) + sink_weight)
-            prob = weight * inverse
-            term = prob * dp
-            delta = jnp.sum(term, axis=0, keepdims=True)
-            prob16 = prob.astype(BF16)
-            slope16 = (term - prob * delta).astype(BF16)
-            prob_own, slope_own = prob16 * own16, slope16 * own16
-            prob2[:WINDOW, wide(index)] = prob_own
-            prob2[WINDOW:, wide(index)] = prob16 - prob_own
-            slope2[:WINDOW, wide(index)] = slope_own
-            slope2[WINDOW:, wide(index)] = slope16 - slope_own
+            inverse = 1.0 / (jnp.sum(edge + whole, axis=0, keepdims=True) + sink_weight)
+            edge, whole = edge * inverse, whole * inverse
+            term_edge, term_whole = edge * dp_edge, whole * dp_whole
+            delta = jnp.sum(term_edge + term_whole, axis=0, keepdims=True)
+            for target, at_edge, at_whole in (
+                (prob2, edge, whole),
+                (slope2, term_edge - edge * delta, term_whole - whole * delta),
+            ):
+                edge16 = at_edge.astype(BF16)
+                edge_own = edge16 * own16
+                target[:HALF, wide(index)] = edge_own
+                target[HALF : 2 * HALF, wide(index)] = edge16 - edge_own
+                target[2 * HALF :, wide(index)] = at_whole.astype(BF16)
             sink_term = sink_weight * inverse * delta
-            sink_rows[row : row + 1] += sink_term[:, :WINDOW]
-            sink_rows[row + 1 : row + 2] += sink_term[:, WINDOW:]
+            for place, lanes in enumerate((slice(0, 128), slice(128, 256))):
+                part = sink_term[:, lanes]
+                sink_rows[row + place : row + place + 1] += jnp.where(left, part, 0.0)
+                sink_rows[row + place + 2 : row + place + 3] += jnp.where(left, 0.0, part)
 
         def finish(index):
-            for source, turned, out_ref in ((prob2, turned_v, o_ref), (slope2, turned_k, dq_ref)):
+            half = items[index][1]
+            rows, left_lanes, right_lanes = corner(index)
+            for source, across, out_ref in ((prob2, turned_v, o_ref), (slope2, turned_k, dq_ref)):
                 out_t = jnp.dot(
-                    turned[feats(index)], source[:, wide(index)], preferred_element_type=F32
+                    across[half][feats(index)], source[:, wide(index)], preferred_element_type=F32
                 ).astype(BF16)
-                out_ref[:, columns(index)] = jnp.concatenate(
-                    [out_t[:, :128], out_t[:, 128:]], axis=0
-                ).T
+                out = jnp.concatenate([out_t[:, :128], out_t[:, 128:]], axis=0).T
+                out_ref[rows, left_lanes] = out[:HALF]
+                out_ref[rows, right_lanes] = out[HALF:]
 
         def reduce(unit):
-            lanes = slice(unit * couples * 256, (unit + 1) * couples * 256)
-            dk = lax.dot_general(
-                slope2[:, lanes], q_turned[:, lanes], turn, preferred_element_type=F32
-            )
-            dv = lax.dot_general(
-                prob2[:, lanes], g_turned[:, lanes], turn, preferred_element_type=F32
-            )
-            return dk * FACTOR, dv
-
-        total = 2 * couples
+            totals = []
+            for weights, rows in ((slope2, q_turned), (prob2, g_turned)):
+                first_half, second_half = (
+                    lax.dot_general(
+                        weights[:, at : at + 512],
+                        rows[:, at : at + 512],
+                        turn,
+                        preferred_element_type=F32,
+                    )
+                    for at in (unit * 1024, unit * 1024 + 512)
+                )
+                totals.append(
+                    jnp.concatenate(
+                        [
+                            first_half[:HALF] + second_half[2 * HALF :],
+                            second_half[:HALF],
+                            first_half[HALF : 2 * HALF],
+                            first_half[2 * HALF :] + second_half[HALF : 2 * HALF],
+                        ],
+                        axis=0,
+                    )
+                )
+            return totals[0] * FACTOR, totals[1]
+
+        total = len(items)
         ahead = {0: products(0)}
         grads = []
         for index in range(total):
@@ -291,7 +339,7 @@
             weigh(index, *ahead.pop(index))
             if index >= 1:
                 finish(index - 1)
-            if index == couples:
+            if index == total // 2:
                 grads.append(reduce(0))
         finish(total - 1)
         grads.append(reduce(1))
@@ -413,6 +461,10 @@
     def shape(dims, kind=BF16):
         return jax.ShapeDtypeStruct(dims, kind)
 
+    queries, out_grad, key_states, value_states, sink_logits = (
+        pltpu.with_memory_space_constraint(value, pltpu.HBM)
+        for value in (queries, out_grad, key_states, value_states, sink_logits)
+    )
     table = jnp.concatenate([branch_start, branch_len, parent_list[:, 0], parent_list[:, 1]])
     *slots, halo_out = pl.pallas_call(
         pack_kernel,
@@ -429,6 +481,7 @@
         name="pack",
     )(sink_logits, key_states, value_states)
     spread = swap(slots, "head")
+    halo = shift(halo_out, "head", 1)
     *chosen, sinks = pl.pallas_call(
         functools.partial(choose_kernel, tok_count, blocks),
         out_shape=(shape((WINDOW, width)),) * LAG + (shape((KV_HEADS * GROUP, 128), F32),),
@@ -438,8 +491,6 @@
         name="choose",
     )(table, *spread)
     arrived = [shift(chosen[s - 1], "tok", s) for s in range(LAG, 0, -1)][::-1]
-    halo_out, _ = lax.optimization_barrier((halo_out, chosen[0]))
-    halo = shift(halo_out, "head", 1)
     quarter = pl.pallas_call(
         functools.partial(arrive_kernel, tok_count),
         out_shape=shape((WINDOW, width)),
@@ -482,8 +533,8 @@
             pltpu.VMEM((2 * GROUP, WINDOW), F32),
             pltpu.VMEM((HEAD_DIM, 2048), BF16),
             pltpu.VMEM((HEAD_DIM, 2048), BF16),
-            pltpu.VMEM((2 * WINDOW, 2048), BF16),
-            pltpu.VMEM((2 * WINDOW, 2048), BF16),
+            pltpu.VMEM((3 * HALF, 2048), BF16),
+            pltpu.VMEM((3 * HALF, 2048), BF16),
         ],
         compiler_params=PARAMS,
         name="attend",
@@ -498,7 +549,6 @@
         name="gather",
     )(*parts)
     returned = [ring(quarter_grad, "tok", -s) for s in range(LAG, 0, -1)][::-1]
-    dhalo, _ = lax.optimization_barrier((dhalo, quarter_grad))
     halo_back = shift(dhalo, "head", -1)
     *landed, sink_near = pl.pallas_call(
         functools.partial(land_kernel, tok_count, blocks),

time: 87.8 us -> 74.7 us (0.85)
  the two profiles are of different devices: /device:TPU:3 before, /device:TPU:1 now
where the time goes in v2:
time: 74.7 us; the launch traced here: 74.3 us
  starting transfers between devices  40.1 us (54%)
  Pallas kernels  18.3 us (24%)
  waiting for transfers between devices  13.6 us (18%)
  local copies, waits for them, and re-layouts  0.76 us (1%)
  other arithmetic  0.75 us (1%)
  between operations  0.75 us (1%)
    ppermute x16, starting transfers between devices, ring(): lax.ppermute(value, axis, [(source, (source + steps) % count) for source...  22.3 us
    ppermute x5, starting transfers between devices, shift(): lax.ppermute(value, axis, [(source, source + steps) for source in range(l...  17.8 us
    pallas_call x1, Pallas kernels, local(): pl.pallas_call(functools.partial(attend_kernel, tok_count, blocks_here, h...  14 us
    ppermute x16, waiting for transfers between devices, ring(): lax.ppermute(value, axis, [(source, (source + steps) % count) for source...  12.3 us
  transfers between devices with their start and end apart: 21, of which 12 were waited for; matrix products, arithmetic and copies ran while one was open for 2% of the time, Pallas kernels for 3%

profile of v2, /device:TPU:1, one launch (start us, length us, event | category | flops | bytes accessed | tf_op | source)
XLA Modules:
  0.0 74.3 jit_solution(303940086720196318)
XLA Ops:
  0.6 1.2 %pack.1 = (bf16[272,256]{1,0:T(8,128)(2,1)S(1)}, bf16[272,256]{1,0:T(8,128)(2,1)S(1)}, bf16[272,256]{1,0:T(8,128)(2,1)S(1)}, bf16[272,256]{1,0:T(8,128)(2,1)S(1)}, bf16[4,128,256]{2,1,0:T(8,128)(2,1)S(1)}) custom-call(f32[16]{0:T(128)} %sink_hbm.1, bf16[256,512]{1,0:T(8,128)(2,1)} %k_ref.1, bf16[256,512]{1,0:T(8,128)(2,1)} %v_ref.1), custom_call_target="tpu_custom_call" | custom-call | tf_op jit(solution)/shard_map/pack/pallas_call | solution.py:469
  1.8 2.7 %collective-permute-start = (bf16[272,256]{1,0:T(8,128)(2,1)S(1)}, bf16[272,256]{1,0:T(8,128)(2,1)S(1)}, u32[]{:S(2)}, u32[]{:S(2)}) collective-permute-start(bf16[272,256]{1,0:T(8,128)(2,1)S(1)} %get-tuple-element.32), channel_id=1, source_target_pairs={{0,1},{1,2},{2,3},{3,0},{4,5},{5,6},{6,7},{7,4},{8,9},{9,10},{10,1... | collective-permute-start | bytes 417800 | tf_op jit(solution)/shard_map/ppermute | solution.py:38
  5.0 3.2 %collective-permute-start.3 = (bf16[4,128,256]{2,1,0:T(8,128)(2,1)S(1)}, bf16[4,128,256]{2,1,0:T(8,128)(2,1)S(1)}, u32[]{:S(2)}, u32[]{:S(2)}) collective-permute-start(bf16[4,128,256]{2,1,0:T(8,128)(2,1)S(1)} %get-tuple-element.36), channel_id=1, source_target_pairs={{0,1},{1,2},{2,3},{4,5},{5,6},{6,7},{8,9},{9,10},{10,11},{12,13},{... | collective-permute-start | bytes 786440 | tf_op jit(solution)/shard_map/ppermute | solution.py:33
  8.2 0.8 %slice_bitcast_fusion.1 = (s32[16]{0:T(128)S(1)}, s32[16]{0:T(128)S(1)}) fusion(s32[16,2]{0,1:T(2,128)} %param.15), kind=kLoop, calls=%fused_computation.2 | loop fusion | bytes 256 | tf_op jit(solution)/shard_map/squeeze | solution.py:468
  8.9 0.7 %pad_add_fusion.table = s32[64]{0:T(128)S(1)} fusion(s32[16]{0:T(128)S(1)} %get-tuple-element.58, s32[16]{0:T(128)S(1)} %get-tuple-element.57, s32[16]{0:T(128)} %param.14, s32[16]{0:T(128)} %param.13), kind=kLoop, calls=%fused_computation | loop fusion | flops 192 | bytes 512 | tf_op jit(solution)/shard_map/concatenate | solution.py:468
  10.8 0.8 %choose.1 = (bf16[128,256]{1,0:T(8,128)(2,1)S(1)}, bf16[128,256]{1,0:T(8,128)(2,1)S(1)}, bf16[128,256]{1,0:T(8,128)(2,1)S(1)}, f32[64,128]{1,0:T(8,128)S(1)}) custom-call(s32[64]{0:T(128)S(1)} %pad_add_fusion.table, bf16[272,256]{1,0:T(8,128)(2,1)S(1)} %get-tuple-element.31.refs_0_, bf16[272,256]{1,0:T(8,128)(2,1)S(1)} %collective-permute-done.refs_1_, ...), custom_call_target="tpu_custom_call" | custom-call | tf_op jit(solution)/shard_map/choose/pallas_call | solution.py:485
  11.7 3.9 %collective-permute-start.4 = (bf16[128,256]{1,0:T(8,128)(2,1)S(1)}, bf16[128,256]{1,0:T(8,128)(2,1)S(1)}, u32[]{:S(2)}, u32[]{:S(2)}) collective-permute-start(bf16[128,256]{1,0:T(8,128)(2,1)S(1)} %get-tuple-element.37), channel_id=1, source_target_pairs={{0,4},{4,8},{8,12},{12,16},{16,20},{20,24},{24,28},{1,5},{5,9},{9,... | collective-permute-start | bytes 196616 | tf_op jit(solution)/shard_map/ppermute | solution.py:33
  15.6 3.2 %collective-permute-start.5 = (bf16[128,256]{1,0:T(8,128)(2,1)S(1)}, bf16[128,256]{1,0:T(8,128)(2,1)S(1)}, u32[]{:S(2)}, u32[]{:S(2)}) collective-permute-start(bf16[128,256]{1,0:T(8,128)(2,1)S(1)} %get-tuple-element.38), channel_id=1, source_target_pairs={{0,8},{4,12},{8,16},{12,20},{16,24},{20,28},{1,9},{5,13},{9,17},{1... | collective-permute-start | bytes 196616 | tf_op jit(solution)/shard_map/ppermute | solution.py:33
  18.8 4.2 %collective-permute-start.6 = (bf16[128,256]{1,0:T(8,128)(2,1)S(1)}, bf16[128,256]{1,0:T(8,128)(2,1)S(1)}, u32[]{:S(2)}, u32[]{:S(2)}) collective-permute-start(bf16[128,256]{1,0:T(8,128)(2,1)S(1)} %get-tuple-element.39), channel_id=1, source_target_pairs={{0,12},{4,16},{8,20},{12,24},{16,28},{1,13},{5,17},{9,21},{13,25},... | collective-permute-start | bytes 196616 | tf_op jit(solution)/shard_map/ppermute | solution.py:33
  23.0 1.3 %collective-permute-done.6.refs_2_ = bf16[128,256]{1,0:T(8,128)(2,1)S(1)} collective-permute-done((bf16[128,256]{1,0:T(8,128)(2,1)S(1)}, bf16[128,256]{1,0:T(8,128)(2,1)S(1)}, u32[]{:S(2)}, u32[]{:S(2)}) %collective-permute-start.6) | collective-permute-done | bytes 65568 | tf_op jit(solution)/shard_map/ppermute | solution.py:33
  24.9 1.8 %collective-permute-start.9 = (bf16[128,256]{1,0:T(8,128)(2,1)S(1)}, bf16[128,256]{1,0:T(8,128)(2,1)S(1)}, u32[]{:S(2)}, u32[]{:S(2)}) collective-permute-start(bf16[128,256]{1,0:T(8,128)(2,1)S(1)} %arrive.1.refs_0_), channel_id=1, source_target_pairs={{0,3},{1,0},{2,1},{3,2},{4,7},{5,4},{6,5},{7,6},{8,11},{9,8},{10,9... | collective-permute-start | bytes 196616 | tf_op jit(solution)/shard_map/ppermute | solution.py:38
  27.1 1.9 %collective-permute-start.7 = (bf16[128,256]{1,0:T(8,128)(2,1)S(1)}, bf16[128,256]{1,0:T(8,128)(2,1)S(1)}, u32[]{:S(2)}, u32[]{:S(2)}) collective-permute-start(bf16[128,256]{1,0:T(8,128)(2,1)S(1)} %arrive.1.refs_0_), channel_id=1, source_target_pairs={{0,1},{1,2},{2,3},{3,0},{4,5},{5,6},{6,7},{7,4},{8,9},{9,10},{10,1... | collective-permute-start | bytes 196616 | tf_op jit(solution)/shard_map/ppermute | solution.py:38
  30.4 14.0 %attend.1 = (bf16[256,4096]{1,0:T(8,128)(2,1)}, bf16[256,4096]{1,0:T(8,128)(2,1)}, f32[256,512]{1,0:T(8,128)S(1)}, f32[256,512]{1,0:T(8,128)S(1)}, bf16[4,128,25...) custom-call(s32[64]{0:T(128)S(1)} %pad_add_fusion.table, ...), custom_call_target="tpu_custom_call" | custom-call | tf_op jit(solution)/shard_map/attend/pallas_call | solution.py:508
  44.5 5.9 %collective-permute-start.11 = (bf16[144,256]{1,0:T(8,128)(2,1)S(1)}, bf16[144,256]{1,0:T(8,128)(2,1)S(1)}, u32[]{:S(2)}, u32[]{:S(2)}) collective-permute-start(bf16[144,256]{1,0:T(8,128)(2,1)S(1)} %get-tuple-element.46), channel_id=1, source_target_pairs={{0,1},{1,2},{2,3},{3,0},{4,5},{5,6},{6,7},{7,4},{8,9},{9,10},{10,1... | collective-permute-start | bytes 221192 | tf_op jit(solution)/shard_map/ppermute | solution.py:38
  50.8 3.3 %collective-permute-start.10 = (bf16[4,128,256]{2,1,0:T(8,128)(2,1)S(1)}, bf16[4,128,256]{2,1,0:T(8,128)(2,1)S(1)}, u32[]{:S(2)}, u32[]{:S(2)}) collective-permute-start(bf16[4,128,256]{2,1,0:T(8,128)(2,1)S(1)} %get-tuple-element.44), channel_id=1, source_target_pairs={{1,0},{2,1},{3,2},{5,4},{6,5},{7,6},{9,8},{10,9},{11,10},{13,12},{... | collective-permute-start | bytes 786440 | tf_op jit(solution)/shard_map/ppermute | solution.py:33
  54.4 2.9 %collective-permute-start.16 = (bf16[144,256]{1,0:T(8,128)(2,1)S(1)}, bf16[144,256]{1,0:T(8,128)(2,1)S(1)}, u32[]{:S(2)}, u32[]{:S(2)}) collective-permute-start(bf16[144,256]{1,0:T(8,128)(2,1)S(1)} %gather.1.here_ref), channel_id=1, source_target_pairs={{0,20},{4,24},{8,28},{12,0},{16,4},{20,8},{24,12},{28,16},{1,21},{... | collective-permute-start | bytes 221192 | tf_op jit(solution)/shard_map/ppermute | solution.py:38
  57.3 2.6 %collective-permute-start.15 = (bf16[144,256]{1,0:T(8,128)(2,1)S(1)}, bf16[144,256]{1,0:T(8,128)(2,1)S(1)}, u32[]{:S(2)}, u32[]{:S(2)}) collective-permute-start(bf16[144,256]{1,0:T(8,128)(2,1)S(1)} %gather.1.here_ref), channel_id=1, source_target_pairs={{0,24},{4,28},{8,0},{12,4},{16,8},{20,12},{24,16},{28,20},{1,25},{... | collective-permute-start | bytes 221192 | tf_op jit(solution)/shard_map/ppermute | solution.py:38
  60.4 1.2 %collective-permute-done.15.refs_1_ = bf16[144,256]{1,0:T(8,128)(2,1)S(1)} collective-permute-done((bf16[144,256]{1,0:T(8,128)(2,1)S(1)}, bf16[144,256]{1,0:T(8,128)(2,1)S(1)}, u32[]{:S(2)}, u32[]{:S(2)}) %collective-permute-start.15) | collective-permute-done | bytes 73760 | tf_op jit(solution)/shard_map/ppermute | solution.py:38
  61.7 1.9 %collective-permute-done.14.refs_0_ = bf16[144,256]{1,0:T(8,128)(2,1)S(1)} collective-permute-done((bf16[144,256]{1,0:T(8,128)(2,1)S(1)}, bf16[144,256]{1,0:T(8,128)(2,1)S(1)}, u32[]{:S(2)}, u32[]{:S(2)}) %collective-permute-start.14) | collective-permute-done | bytes 73760 | tf_op jit(solution)/shard_map/ppermute | solution.py:38
  64.3 1.2 %collective-permute-start.18 = (bf16[256,256]{1,0:T(8,128)(2,1)S(1)}, bf16[256,256]{1,0:T(8,128)(2,1)S(1)}, u32[]{:S(2)}, u32[]{:S(2)}) collective-permute-start(bf16[256,256]{1,0:T(8,128)(2,1)S(1)} %get-tuple-element.51), channel_id=1, source_target_pairs={{0,1},{1,2},{2,3},{3,0},{4,5},{5,6},{6,7},{7,4},{8,9},{9,10},{10,1... | collective-permute-start | bytes 393224 | tf_op jit(solution)/shard_map/ppermute | solution.py:38
  65.5 1.3 %collective-permute-start.19 = (bf16[256,256]{1,0:T(8,128)(2,1)S(1)}, bf16[256,256]{1,0:T(8,128)(2,1)S(1)}, u32[]{:S(2)}, u32[]{:S(2)}) collective-permute-start(bf16[256,256]{1,0:T(8,128)(2,1)S(1)} %get-tuple-element.52), channel_id=1, source_target_pairs={{0,2},{1,3},{2,0},{3,1},{4,6},{5,7},{6,4},{7,5},{8,10},{9,11},{10,... | collective-permute-start | bytes 393224 | tf_op jit(solution)/shard_map/ppermute | solution.py:38
  67.3 2.8 %collective-permute-done.17.far_ref = f32[8,128]{1,0:T(8,128)S(1)} collective-permute-done((f32[8,128]{1,0:T(8,128)S(1)}, f32[8,128]{1,0:T(8,128)S(1)}, u32[]{:S(2)}, u32[]{:S(2)}) %collective-permute-start.17) | collective-permute-done | bytes 4128 | tf_op jit(solution)/shard_map/ppermute | solution.py:38
  70.1 2.6 %collective-permute-done.19.refs_2_ = bf16[256,256]{1,0:T(8,128)(2,1)S(1)} collective-permute-done((bf16[256,256]{1,0:T(8,128)(2,1)S(1)}, bf16[256,256]{1,0:T(8,128)(2,1)S(1)}, u32[]{:S(2)}, u32[]{:S(2)}) %collective-permute-start.19) | collective-permute-done | bytes 131104 | tf_op jit(solution)/shard_map/ppermute | solution.py:38
  73.3 1.0 %total.1 = (bf16[256,512]{1,0:T(8,128)(2,1)}, bf16[256,512]{1,0:T(8,128)(2,1)}, f32[16]{0:T(128)}) custom-call(f32[256,512]{1,0:T(8,128)S(1)} %get-tuple-element.42.dk_ref, f32[256,512]{1,0:T(8,128)S(1)} %get-tuple-element.43.dv_ref, bf16[4,128,256]{2,1,0:T(8,128)(2,1)S(1)} %collective-permute-done.10.halo_ref, f32[8,128]{1,0:T(8,128)S(1)} %get-tuple-element.49.sink_ref, ...), custom_call_target="tpu_custom_call" | custom-call | tf_op jit(solution)/shard_map/total/pallas_call | solution.py:567
  (27 shorter events, 7.2 us)
Async XLA Ops:
  1.8 7.9 %collective-permute-start = (bf16[272,256]{1,0:T(8,128)(2,1)S(1)}, bf16[272,256]{1,0:T(8,128)(2,1)S(1)}, u32[]{:S(2)}, u32[]{:S(2)}) collective-permute-start(bf16[272,256]{1,0:T(8,128)(2,1)S(1)} %get-tuple-element.32), channel_id=1, source_target_pairs={{0,1},{1,2},{2,3},{3,0},{4,5},{5,6},{6,7},{7,4},{8,9},{9,10},{10,1... | collective-permute-start | bytes 417800 | tf_op jit(solution)/shard_map/ppermute | solution.py:38
  4.5 5.9 %collective-permute-start.1 = (bf16[272,256]{1,0:T(8,128)(2,1)S(1)}, bf16[272,256]{1,0:T(8,128)(2,1)S(1)}, u32[]{:S(2)}, u32[]{:S(2)}) collective-permute-start(bf16[272,256]{1,0:T(8,128)(2,1)S(1)} %get-tuple-element.33), channel_id=1, source_target_pairs={{0,2},{1,3},{2,0},{3,1},{4,6},{5,7},{6,4},{7,5},{8,10},{9,11},{10,... | collective-permute-start | bytes 417800 | tf_op jit(solution)/shard_map/ppermute | solution.py:38
  4.5 6.4 %collective-permute-start.2 = (bf16[272,256]{1,0:T(8,128)(2,1)S(1)}, bf16[272,256]{1,0:T(8,128)(2,1)S(1)}, u32[]{:S(2)}, u32[]{:S(2)}) collective-permute-start(bf16[272,256]{1,0:T(8,128)(2,1)S(1)} %get-tuple-element.34), channel_id=1, source_target_pairs={{0,3},{1,0},{2,1},{3,2},{4,7},{5,4},{6,5},{7,6},{8,11},{9,8},{10,9... | collective-permute-start | bytes 417800 | tf_op jit(solution)/shard_map/ppermute | solution.py:38
  5.0 24.1 %collective-permute-start.3 = (bf16[4,128,256]{2,1,0:T(8,128)(2,1)S(1)}, bf16[4,128,256]{2,1,0:T(8,128)(2,1)S(1)}, u32[]{:S(2)}, u32[]{:S(2)}) collective-permute-start(bf16[4,128,256]{2,1,0:T(8,128)(2,1)S(1)} %get-tuple-element.36), channel_id=1, source_target_pairs={{0,1},{1,2},{2,3},{4,5},{5,6},{6,7},{8,9},{9,10},{10,11},{12,13},{... | collective-permute-start | bytes 786440 | tf_op jit(solution)/shard_map/ppermute | solution.py:33
  11.7 11.3 %collective-permute-start.4 = (bf16[128,256]{1,0:T(8,128)(2,1)S(1)}, bf16[128,256]{1,0:T(8,128)(2,1)S(1)}, u32[]{:S(2)}, u32[]{:S(2)}) collective-permute-start(bf16[128,256]{1,0:T(8,128)(2,1)S(1)} %get-tuple-element.37), channel_id=1, source_target_pairs={{0,4},{4,8},{8,12},{12,16},{16,20},{20,24},{24,28},{1,5},{5,9},{9,... | collective-permute-start | bytes 196616 | tf_op jit(solution)/shard_map/ppermute | solution.py:33
  15.6 7.4 %collective-permute-start.5 = (bf16[128,256]{1,0:T(8,128)(2,1)S(1)}, bf16[128,256]{1,0:T(8,128)(2,1)S(1)}, u32[]{:S(2)}, u32[]{:S(2)}) collective-permute-start(bf16[128,256]{1,0:T(8,128)(2,1)S(1)} %get-tuple-element.38), channel_id=1, source_target_pairs={{0,8},{4,12},{8,16},{12,20},{16,24},{20,28},{1,9},{5,13},{9,17},{1... | collective-permute-start | bytes 196616 | tf_op jit(solution)/shard_map/ppermute | solution.py:33
  18.8 5.5 %collective-permute-start.6 = (bf16[128,256]{1,0:T(8,128)(2,1)S(1)}, bf16[128,256]{1,0:T(8,128)(2,1)S(1)}, u32[]{:S(2)}, u32[]{:S(2)}) collective-permute-start(bf16[128,256]{1,0:T(8,128)(2,1)S(1)} %get-tuple-element.39), channel_id=1, source_target_pairs={{0,12},{4,16},{8,20},{12,24},{16,28},{1,13},{5,17},{9,21},{13,25},... | collective-permute-start | bytes 196616 | tf_op jit(solution)/shard_map/ppermute | solution.py:33
  24.9 4.2 %collective-permute-start.9 = (bf16[128,256]{1,0:T(8,128)(2,1)S(1)}, bf16[128,256]{1,0:T(8,128)(2,1)S(1)}, u32[]{:S(2)}, u32[]{:S(2)}) collective-permute-start(bf16[128,256]{1,0:T(8,128)(2,1)S(1)} %arrive.1.refs_0_), channel_id=1, source_target_pairs={{0,3},{1,0},{2,1},{3,2},{4,7},{5,4},{6,5},{7,6},{8,11},{9,8},{10,9... | collective-permute-start | bytes 196616 | tf_op jit(solution)/shard_map/ppermute | solution.py:38
  26.7 3.1 %collective-permute-start.8 = (bf16[128,256]{1,0:T(8,128)(2,1)S(1)}, bf16[128,256]{1,0:T(8,128)(2,1)S(1)}, u32[]{:S(2)}, u32[]{:S(2)}) collective-permute-start(bf16[128,256]{1,0:T(8,128)(2,1)S(1)} %arrive.1.refs_0_), channel_id=1, source_target_pairs={{0,2},{1,3},{2,0},{3,1},{4,6},{5,7},{6,4},{7,5},{8,10},{9,11},{10,... | collective-permute-start | bytes 196616 | tf_op jit(solution)/shard_map/ppermute | solution.py:38
  27.1 3.3 %collective-permute-start.7 = (bf16[128,256]{1,0:T(8,128)(2,1)S(1)}, bf16[128,256]{1,0:T(8,128)(2,1)S(1)}, u32[]{:S(2)}, u32[]{:S(2)}) collective-permute-start(bf16[128,256]{1,0:T(8,128)(2,1)S(1)} %arrive.1.refs_0_), channel_id=1, source_target_pairs={{0,1},{1,2},{2,3},{3,0},{4,5},{5,6},{6,7},{7,4},{8,9},{9,10},{10,1... | collective-permute-start | bytes 196616 | tf_op jit(solution)/shard_map/ppermute | solution.py:38
  44.5 9.7 %collective-permute-start.11 = (bf16[144,256]{1,0:T(8,128)(2,1)S(1)}, bf16[144,256]{1,0:T(8,128)(2,1)S(1)}, u32[]{:S(2)}, u32[]{:S(2)}) collective-permute-start(bf16[144,256]{1,0:T(8,128)(2,1)S(1)} %get-tuple-element.46), channel_id=1, source_target_pairs={{0,1},{1,2},{2,3},{3,0},{4,5},{5,6},{6,7},{7,4},{8,9},{9,10},{10,1... | collective-permute-start | bytes 221192 | tf_op jit(solution)/shard_map/ppermute | solution.py:38
  50.4 3.8 %collective-permute-start.12 = (bf16[144,256]{1,0:T(8,128)(2,1)S(1)}, bf16[144,256]{1,0:T(8,128)(2,1)S(1)}, u32[]{:S(2)}, u32[]{:S(2)}) collective-permute-start(bf16[144,256]{1,0:T(8,128)(2,1)S(1)} %get-tuple-element.47), channel_id=1, source_target_pairs={{0,2},{1,3},{2,0},{3,1},{4,6},{5,7},{6,4},{7,5},{8,10},{9,11},{10,... | collective-permute-start | bytes 221192 | tf_op jit(solution)/shard_map/ppermute | solution.py:38
  50.4 4.0 %collective-permute-start.13 = (bf16[144,256]{1,0:T(8,128)(2,1)S(1)}, bf16[144,256]{1,0:T(8,128)(2,1)S(1)}, u32[]{:S(2)}, u32[]{:S(2)}) collective-permute-start(bf16[144,256]{1,0:T(8,128)(2,1)S(1)} %get-tuple-element.48), channel_id=1, source_target_pairs={{0,3},{1,0},{2,1},{3,2},{4,7},{5,4},{6,5},{7,6},{8,11},{9,8},{10,9... | collective-permute-start | bytes 221192 | tf_op jit(solution)/shard_map/ppermute | solution.py:38
  50.8 19.3 %collective-permute-start.10 = (bf16[4,128,256]{2,1,0:T(8,128)(2,1)S(1)}, bf16[4,128,256]{2,1,0:T(8,128)(2,1)S(1)}, u32[]{:S(2)}, u32[]{:S(2)}) collective-permute-start(bf16[4,128,256]{2,1,0:T(8,128)(2,1)S(1)} %get-tuple-element.44), channel_id=1, source_target_pairs={{1,0},{2,1},{3,2},{5,4},{6,5},{7,6},{9,8},{10,9},{11,10},{13,12},{... | collective-permute-start | bytes 786440 | tf_op jit(solution)/shard_map/ppermute | solution.py:33
  54.4 6.0 %collective-permute-start.16 = (bf16[144,256]{1,0:T(8,128)(2,1)S(1)}, bf16[144,256]{1,0:T(8,128)(2,1)S(1)}, u32[]{:S(2)}, u32[]{:S(2)}) collective-permute-start(bf16[144,256]{1,0:T(8,128)(2,1)S(1)} %gather.1.here_ref), channel_id=1, source_target_pairs={{0,20},{4,24},{8,28},{12,0},{16,4},{20,8},{24,12},{28,16},{1,21},{... | collective-permute-start | bytes 221192 | tf_op jit(solution)/shard_map/ppermute | solution.py:38
  57.3 4.4 %collective-permute-start.15 = (bf16[144,256]{1,0:T(8,128)(2,1)S(1)}, bf16[144,256]{1,0:T(8,128)(2,1)S(1)}, u32[]{:S(2)}, u32[]{:S(2)}) collective-permute-start(bf16[144,256]{1,0:T(8,128)(2,1)S(1)} %gather.1.here_ref), channel_id=1, source_target_pairs={{0,24},{4,28},{8,0},{12,4},{16,8},{20,12},{24,16},{28,20},{1,25},{... | collective-permute-start | bytes 221192 | tf_op jit(solution)/shard_map/ppermute | solution.py:38
  59.9 3.6 %collective-permute-start.14 = (bf16[144,256]{1,0:T(8,128)(2,1)S(1)}, bf16[144,256]{1,0:T(8,128)(2,1)S(1)}, u32[]{:S(2)}, u32[]{:S(2)}) collective-permute-start(bf16[144,256]{1,0:T(8,128)(2,1)S(1)} %gather.1.here_ref), channel_id=1, source_target_pairs={{0,28},{4,0},{8,4},{12,8},{16,12},{20,16},{24,20},{28,24},{1,29},{... | collective-permute-start | bytes 221192 | tf_op jit(solution)/shard_map/ppermute | solution.py:38
  64.3 5.9 %collective-permute-start.18 = (bf16[256,256]{1,0:T(8,128)(2,1)S(1)}, bf16[256,256]{1,0:T(8,128)(2,1)S(1)}, u32[]{:S(2)}, u32[]{:S(2)}) collective-permute-start(bf16[256,256]{1,0:T(8,128)(2,1)S(1)} %get-tuple-element.51), channel_id=1, source_target_pairs={{0,1},{1,2},{2,3},{3,0},{4,5},{5,6},{6,7},{7,4},{8,9},{9,10},{10,1... | collective-permute-start | bytes 393224 | tf_op jit(solution)/shard_map/ppermute | solution.py:38
  65.5 7.2 %collective-permute-start.19 = (bf16[256,256]{1,0:T(8,128)(2,1)S(1)}, bf16[256,256]{1,0:T(8,128)(2,1)S(1)}, u32[]{:S(2)}, u32[]{:S(2)}) collective-permute-start(bf16[256,256]{1,0:T(8,128)(2,1)S(1)} %get-tuple-element.52), channel_id=1, source_target_pairs={{0,2},{1,3},{2,0},{3,1},{4,6},{5,7},{6,4},{7,5},{8,10},{9,11},{10,... | collective-permute-start | bytes 393224 | tf_op jit(solution)/shard_map/ppermute | solution.py:38
  66.7 6.6 %collective-permute-start.20 = (bf16[256,256]{1,0:T(8,128)(2,1)S(1)}, bf16[256,256]{1,0:T(8,128)(2,1)S(1)}, u32[]{:S(2)}, u32[]{:S(2)}) collective-permute-start(bf16[256,256]{1,0:T(8,128)(2,1)S(1)} %get-tuple-element.53), channel_id=1, source_target_pairs={{0,3},{1,0},{2,1},{3,2},{4,7},{5,4},{6,5},{7,6},{8,11},{9,8},{10,9... | collective-permute-start | bytes 393224 | tf_op jit(solution)/shard_map/ppermute | solution.py:38
  66.7 3.4 %collective-permute-start.17 = (f32[8,128]{1,0:T(8,128)S(1)}, f32[8,128]{1,0:T(8,128)S(1)}, u32[]{:S(2)}, u32[]{:S(2)}) collective-permute-start(f32[8,128]{1,0:T(8,128)S(1)} %get-tuple-element.49.sink_ref), channel_id=1, source_target_pairs={{0,16},{4,20},{8,24},{12,28},{16,0},{20,4},{24,8},{28,12},{1,17},{... | collective-permute-start | bytes 12296 | tf_op jit(solution)/shard_map/ppermute | solution.py:38
